TPU v7x, 512 devices: a whole 4x4x16 slice. The times are simulated.
512 devices in a mesh: dp: 16 (over y, z_hi), row: 8 (over x, core), col: 4 (over z_lo).
Axes of the slice: x: 4, y: 4, z: 16 (z_hi: 4, z_lo: 4; z = z_hi * 4 + z_lo), core: 2. Of those that a mesh axis runs over, the one named last changes fastest.
Arguments:
- features: bfloat16 [16, 160, 160, 640], P('dp', 'row', 'col'), may hold values from -800 to 800
- hole_mask: int32 [16, 160, 160], P('dp', 'row', 'col'), may hold values 0 or 1
- norm_gain: float32 [640], replicated, may hold values from 0.5 to 1.5
- norm_shift: float32 [640], replicated, may hold values from -3 to 3
- conv_weight: bfloat16 [9, 640, 640], P(None, 'dp'), may hold values from -0.078125 to 0.078125
- mask_weight: float32 [9, 640], replicated, may hold values from -3 to 3
- conv_bias: float32 [640], replicated, may hold values from -3 to 3
Outputs:
- conv_out: bfloat16 [16, 160, 160, 640], P('dp', 'row', 'col')
All inputs are finite; a program needn't handle non-finite values. No bound on the sum of `hole_mask` on one device may be relied on, other than what follows from the above.
Results may differ from a plain program's by a relative error of at most 0.0032.
Values may be sent and summed in bfloat16 or wider, within the bound.
A program may use at most 128 MiB of HBM per device.

v0:
```python
import jax
import jax.numpy as jnp
from jax import lax
from jax.sharding import PartitionSpec as P

GROUPS = 32


EPS = 1e-05


def with_halo(cells, sides, width):
    for axis, dim in sides:
        count = lax.axis_size(axis)
        ends = count - 1
        head = lax.slice_in_dim(cells, 0, width, axis=dim)
        tail = lax.slice_in_dim(cells, cells.shape[dim] - width, cells.shape[dim], axis=dim)
        cells = jnp.concatenate(
            [
                lax.ppermute(tail, axis, [(i, (i + 1) % count) for i in range(ends)]),
                cells,
                lax.ppermute(head, axis, [((i + 1) % count, i) for i in range(ends)]),
            ],
            axis=dim,
        )
    return cells


def local(features, hole_mask, norm_gain, norm_shift, conv_weight, mask_weight, conv_bias):
    rows_here = features.shape[1]
    cols_here = features.shape[2]
    channels = features.shape[3]
    cells = rows_here * cols_here
    count = cells * (channels // GROUPS) * lax.axis_size("row") * lax.axis_size("col")
    grouped = (
        features[0].astype(jnp.float32).reshape(rows_here, cols_here, GROUPS, channels // GROUPS)
    )
    sums = lax.psum(jnp.sum(grouped, axis=(0, 1, 3)), ("row", "col"))
    mean_val = sums / count
    deviate = grouped - mean_val[None, None, :, None]
    squares = lax.psum(jnp.sum(deviate * deviate, axis=(0, 1, 3)), ("row", "col"))
    var_val = squares / count
    normed = (deviate * lax.rsqrt(var_val + EPS)[None, None, :, None]).reshape(
        rows_here, cols_here, channels
    )
    act_low = jax.nn.silu(normed * norm_gain + norm_shift).astype(jnp.bfloat16)
    padded = with_halo(act_low, (("row", 0), ("col", 1)), 1)
    mask_low = hole_mask[0].astype(jnp.bfloat16)
    mask_pad = with_halo(mask_low, (("row", 0), ("col", 1)), 1).astype(jnp.float32)
    base_term = jnp.zeros((rows_here, cols_here, channels), jnp.float32) + conv_bias
    for tap in range(9):
        row_off = tap // 3
        col_off = tap % 3
        base_term = (
            base_term
            + mask_pad[row_off : row_off + rows_here, col_off : col_off + cols_here, None]
            * mask_weight[tap]
        )

    def window_of(tap):
        row_off = tap // 3
        col_off = tap % 3
        return padded[row_off : row_off + rows_here, col_off : col_off + cols_here]

    piece = lax.all_gather(conv_weight, "dp", axis=1, tiled=True)
    depth = piece.shape[1]
    stacked = jnp.concatenate([window_of(tap).reshape(cells, depth) for tap in range(9)], axis=1)
    total = jnp.dot(
        stacked, piece.reshape(9 * depth, piece.shape[2]), preferred_element_type=jnp.float32
    )
    conv_out = (total.reshape(rows_here, cols_here, channels) + base_term).astype(jnp.bfloat16)
    return conv_out[None]


def solution(mesh):
    in_specs = (
        P("dp", "row", "col", None),
        P("dp", "row", "col"),
        P(),
        P(),
        P(None, "dp", None),
        P(),
        P(),
    )
    out_specs = P("dp", "row", "col", None)
    return jax.shard_map(local, mesh=mesh, in_specs=in_specs, out_specs=out_specs, check_vma=False)
```

profile of v0, /device:TPU:145, one launch (start us, length us, event | category | flops | bytes accessed | tf_op | source)
XLA Modules:
  0.0 281.2 jit_solution(10182453041436015365)
XLA Ops:
  7.3 1.4 convert_reduce_fusion
  8.9 76.2 %psum.14 = f32[32]{0:T(128)S(1)} all-reduce(f32[32]{0:T(128)S(1)} %reduce_sum.25), channel_id=1, replica_groups=mesh['dp'=16,'row'=8,'col'=4] {'row','col'}, use_global_device_ids=true, to_apply=%region_2.0 | all-reduce | flops 32 | bytes 256 | tf_op jit(solution)/shard_map/psum | solution.py:38
  85.9 127.2 %psum.15 = f32[32]{0:T(128)S(1)} all-reduce(f32[32]{0:T(128)S(1)} %reduce_sum.37), channel_id=1, replica_groups=mesh['dp'=16,'row'=8,'col'=4] {'row','col'}, use_global_device_ids=true, to_apply=%region_5.6 | all-reduce | flops 32 | bytes 256 | tf_op jit(solution)/shard_map/psum | solution.py:41
  214.0 8.2 %collective-permute-start = (bf16[1,40,640]{2,1,0:T(8,128)(2,1)S(1)}, bf16[1,40,640]{2,1,0:T(8,128)(2,1)S(1)}, u32[]{:S(2)}, u32[]{:S(2)}) collective-permute-start(bf16[1,40,640]{2,1,0:T(8,128)(2,1)S(1)} %get-tuple-element.18), channel_id=1, source_target_pairs={{0,4},{4,8},{8,12},{12,16},{16,20},{20,24},{24,28},{1,5},{5,9},{9,... | collective-permute-start | bytes 153608 | tf_op jit(solution)/shard_map/ppermute | solution.py:20
  222.2 1.9 collective-permute-start.1
  224.1 3.6 %collective-permute-start.4 = (bf16[1,40]{1,0:T(2,128)(2,1)S(1)}, bf16[1,40]{1,0:T(2,128)(2,1)S(1)}, u32[]{:S(2)}, u32[]{:S(2)}) collective-permute-start(bf16[1,40]{1,0:T(2,128)(2,1)S(1)} %get-tuple-element.29), channel_id=1, source_target_pairs={{0,4},{4,8},{8,12},{12,16},{16,20},{20,24},{24,28},{1,5},{5,9},{9,... | collective-permute-start | bytes 248 | tf_op jit(solution)/shard_map/ppermute | solution.py:20
  227.8 1.9 collective-permute-start.5
  229.8 2.8 %collective-permute-done.5 = bf16[1,40]{1,0:T(2,128)(2,1)S(1)} collective-permute-done((bf16[1,40]{1,0:T(2,128)(2,1)S(1)}, bf16[1,40]{1,0:T(2,128)(2,1)S(1)}, u32[]{:S(2)}, u32[]{:S(2)}) %collective-permute-start.5) | collective-permute-done | bytes 112 | tf_op jit(solution)/shard_map/ppermute | solution.py:22
  232.7 3.9 %collective-permute-start.6 = (bf16[22,1]{1,0:T(8,128)(2,1)S(1)}, bf16[22,1]{1,0:T(8,128)(2,1)S(1)}, u32[]{:S(2)}, u32[]{:S(2)}) collective-permute-start(bf16[22,1]{1,0:T(8,128)(2,1)S(1)} %get-tuple-element.31), channel_id=1, source_target_pairs={{0,1},{1,2},{2,3},{4,5},{5,6},{6,7},{8,9},{9,10},{10,11},{12,13},{... | collective-permute-start | bytes 140 | tf_op jit(solution)/shard_map/ppermute | solution.py:20
  236.6 1.3 collective-permute-start.7
  238.0 3.1 %collective-permute-done.7 = bf16[22,1]{1,0:T(8,128)(2,1)S(1)} collective-permute-done((bf16[22,1]{1,0:T(8,128)(2,1)S(1)}, bf16[22,1]{1,0:T(8,128)(2,1)S(1)}, u32[]{:S(2)}, u32[]{:S(2)}) %collective-permute-start.7) | collective-permute-done | bytes 76 | tf_op jit(solution)/shard_map/ppermute | solution.py:22
  241.2 1.9 collective-permute-start.2
  243.1 1.3 collective-permute-start.3
  244.6 4.3 %collective-permute-done.3 = bf16[22,1,640]{2,1,0:T(2,128)(2,1)S(1)} collective-permute-done((bf16[22,1,640]{2,1,0:T(2,128)(2,1)S(1)}, bf16[22,1,640]{2,1,0:T(2,128)(2,1)S(1)}, u32[]{:S(2)}, u32[]{:S(2)}) %collective-permute-start.3) | collective-permute-done | bytes 28192 | tf_op jit(solution)/shard_map/ppermute | solution.py:22
  249.7 1.1 slice_dynamic-update-slice_fusion.5
  250.8 1.2 fusion.14
  252.0 1.3 slice_dynamic-update-slice_fusion.4
  253.3 1.1 slice_dynamic-update-slice_fusion.3
  254.4 1.7 constant_dynamic-update-slice_fusion
  256.2 1.4 slice_dynamic-update-slice_fusion.2
  257.6 1.1 slice_dynamic-update-slice_fusion.1
  258.6 1.1 fusion.13
  259.8 1.4 slice_dynamic-update-slice_fusion
  261.1 13.2 %fusion.12 = bf16[1,20,40,640]{3,2,1,0:T(8,128)(2,1)} fusion(bf16[20,40,5760]{2,1,0:T(8,128)(2,1)} %slice_dynamic-update-slice_fusion, bf16[5760,640,1]{1,0,2:T(8,128)(2,1)} %bitcast.42, f32[640]{0:T(1024)S(1)} %get-tuple-element.12, f32[20,40]{1,0:T(8,128)S(1)} %get-tuple-element.21, f32[640]{0:T(1024)S(1)} %get-tuple-element.13, ...), kind=kOutput, calls=%fused_computation.16 | convolution fusion | flops 5908480000 | bytes 17667200 | tf_op jit(solution)/shard_map/dot_general | solution.py:68
  (43 shorter events, 3.9 us)
Async XLA Ops:
  6.5 78.8 %copy-start = (bf16[1,20,40,640]{3,2,1,0:T(8,128)(2,1)S(1)}, bf16[1,20,40,640]{3,2,1,0:T(8,128)(2,1)}, u32[]{:S(2)}) copy-start(bf16[1,20,40,640]{3,2,1,0:T(8,128)(2,1)} %param.7) | copy-start | bytes 3072004
  6.5 206.7 %copy-start.1 = (f32[640]{0:T(1024)S(1)}, f32[640]{0:T(1024)}, u32[]{:S(2)}) copy-start(f32[640]{0:T(1024)} %param.10) | copy-start | bytes 7684
  6.5 206.7 %copy-start.2 = (f32[640]{0:T(1024)S(1)}, f32[640]{0:T(1024)}, u32[]{:S(2)}) copy-start(f32[640]{0:T(1024)} %param.9) | copy-start | bytes 7684
  6.5 254.6 %all-gather.2.cloned.1.call-start = ((), (), s32[]{:S(2)}) async-start(), calls=%async_computation | async-start | bytes 7833600 | tf_op jit(solution)/shard_map/all_gather | solution.py:65
  7.3 216.8 %copy-start.4 = (s32[1,20,40]{2,0,1:T(1,128)S(1)}, s32[1,20,40]{2,0,1:T(1,128)}, u32[]{:S(2)}) copy-start(s32[1,20,40]{2,0,1:T(1,128)} %param.8) | copy-start | bytes 9604
  7.3 222.5 %copy-start.3 = (f32[9,640]{1,0:T(8,128)S(1)}, f32[9,640]{1,0:T(8,128)}, u32[]{:S(2)}) copy-start(f32[9,640]{1,0:T(8,128)} %param.12) | copy-start | bytes 69124
  214.0 27.1 %collective-permute-start = (bf16[1,40,640]{2,1,0:T(8,128)(2,1)S(1)}, bf16[1,40,640]{2,1,0:T(8,128)(2,1)S(1)}, u32[]{:S(2)}, u32[]{:S(2)}) collective-permute-start(bf16[1,40,640]{2,1,0:T(8,128)(2,1)S(1)} %get-tuple-element.18), channel_id=1, source_target_pairs={{0,4},{4,8},{8,12},{12,16},{16,20},{20,24},{24,28},{1,5},{5,9},{9,... | collective-permute-start | bytes 153608 | tf_op jit(solution)/shard_map/ppermute | solution.py:20
  222.2 18.9 %collective-permute-start.1 = (bf16[1,40,640]{2,1,0:T(8,128)(2,1)S(1)}, bf16[1,40,640]{2,1,0:T(8,128)(2,1)S(1)}, u32[]{:S(2)}, u32[]{:S(2)}) collective-permute-start(bf16[1,40,640]{2,1,0:T(8,128)(2,1)S(1)} %get-tuple-element.19), channel_id=1, source_target_pairs={{4,0},{8,4},{12,8},{16,12},{20,16},{24,20},{28,24},{5,1},{9,5},{13... | collective-permute-start | bytes 153608 | tf_op jit(solution)/shard_map/ppermute | solution.py:22
  224.1 5.7 %collective-permute-start.4 = (bf16[1,40]{1,0:T(2,128)(2,1)S(1)}, bf16[1,40]{1,0:T(2,128)(2,1)S(1)}, u32[]{:S(2)}, u32[]{:S(2)}) collective-permute-start(bf16[1,40]{1,0:T(2,128)(2,1)S(1)} %get-tuple-element.29), channel_id=1, source_target_pairs={{0,4},{4,8},{8,12},{12,16},{16,20},{20,24},{24,28},{1,5},{5,9},{9,... | collective-permute-start | bytes 248 | tf_op jit(solution)/shard_map/ppermute | solution.py:20
  227.8 4.9 %collective-permute-start.5 = (bf16[1,40]{1,0:T(2,128)(2,1)S(1)}, bf16[1,40]{1,0:T(2,128)(2,1)S(1)}, u32[]{:S(2)}, u32[]{:S(2)}) collective-permute-start(bf16[1,40]{1,0:T(2,128)(2,1)S(1)} %get-tuple-element.30), channel_id=1, source_target_pairs={{4,0},{8,4},{12,8},{16,12},{20,16},{24,20},{28,24},{5,1},{9,5},{13... | collective-permute-start | bytes 248 | tf_op jit(solution)/shard_map/ppermute | solution.py:22
  232.7 5.2 %collective-permute-start.6 = (bf16[22,1]{1,0:T(8,128)(2,1)S(1)}, bf16[22,1]{1,0:T(8,128)(2,1)S(1)}, u32[]{:S(2)}, u32[]{:S(2)}) collective-permute-start(bf16[22,1]{1,0:T(8,128)(2,1)S(1)} %get-tuple-element.31), channel_id=1, source_target_pairs={{0,1},{1,2},{2,3},{4,5},{5,6},{6,7},{8,9},{9,10},{10,11},{12,13},{... | collective-permute-start | bytes 140 | tf_op jit(solution)/shard_map/ppermute | solution.py:20
  236.6 4.4 %collective-permute-start.7 = (bf16[22,1]{1,0:T(8,128)(2,1)S(1)}, bf16[22,1]{1,0:T(8,128)(2,1)S(1)}, u32[]{:S(2)}, u32[]{:S(2)}) collective-permute-start(bf16[22,1]{1,0:T(8,128)(2,1)S(1)} %get-tuple-element.32), channel_id=1, source_target_pairs={{1,0},{2,1},{3,2},{5,4},{6,5},{7,6},{9,8},{10,9},{11,10},{13,12},{... | collective-permute-start | bytes 140 | tf_op jit(solution)/shard_map/ppermute | solution.py:22
  241.2 3.4 %collective-permute-start.2 = (bf16[22,1,640]{2,1,0:T(2,128)(2,1)S(1)}, bf16[22,1,640]{2,1,0:T(2,128)(2,1)S(1)}, u32[]{:S(2)}, u32[]{:S(2)}) collective-permute-start(bf16[22,1,640]{2,1,0:T(2,128)(2,1)S(1)} %get-tuple-element.17), channel_id=1, source_target_pairs={{0,1},{1,2},{2,3},{4,5},{5,6},{6,7},{8,9},{9,10},{10,11},{12,13},{... | collective-permute-start | bytes 84488 | tf_op jit(solution)/shard_map/ppermute | solution.py:20
  243.1 5.7 %collective-permute-start.3 = (bf16[22,1,640]{2,1,0:T(2,128)(2,1)S(1)}, bf16[22,1,640]{2,1,0:T(2,128)(2,1)S(1)}, u32[]{:S(2)}, u32[]{:S(2)}) collective-permute-start(bf16[22,1,640]{2,1,0:T(2,128)(2,1)S(1)} %get-tuple-element.16), channel_id=1, source_target_pairs={{1,0},{2,1},{3,2},{5,4},{6,5},{7,6},{9,8},{10,9},{11,10},{13,12},{... | collective-permute-start | bytes 84488 | tf_op jit(solution)/shard_map/ppermute | solution.py:22
  258.6 2.5 copy-start.5
Sparse Core Ops, SparseCore 0:
  10.4 172.2 all-gather.1
where the time goes:
time: 282 us; the launch traced here: 281 us
  blocking collectives  203 us (72%)
  starting transfers between devices  24.1 us (9%)
  between operations  13.6 us (5%)
  matrix products  13.2 us (5%)
  waiting for transfers between devices  11 us (4%)
  local copies, waits for them, and re-layouts  8.2 us (3%)
  other arithmetic  7.72 us (3%)
    psum x1, blocking collectives, local(): lax.psum(jnp.sum(deviate * deviate, axis=(0, 1, 3)), ('row', 'col'))  127 us
    psum x1, blocking collectives, local(): sums = lax.psum(jnp.sum(grouped, axis=(0, 1, 3)), ('row', 'col'))  76.2 us
    ppermute x4, starting transfers between devices, with_halo(): lax.ppermute(tail, axis, [(i, (i + 1) % count) for i in range(ends)])  17.6 us
    dot_general x1, matrix products, local(): jnp.dot(stacked, piece.reshape(9 * depth, piece.shape[2]), preferred_elem...  13.2 us
    ppermute x4, waiting for transfers between devices, with_halo(): lax.ppermute(head, axis, [((i + 1) % count, i) for i in range(ends)])  10.2 us
    ppermute x4, starting transfers between devices, with_halo(): lax.ppermute(head, axis, [((i + 1) % count, i) for i in range(ends)])  6.43 us
    unnamed x18, local copies, waits for them, and re-layouts  6.05 us
  transfers between devices with their start and end apart: 9, of which 4 were waited for; matrix products, arithmetic and copies ran while one was open for 6% of the time, Pallas kernels for 0%

commit v1 on v0

v1 whole, which is shorter than its diff:
```python
import jax
import jax.numpy as jnp
from jax import lax
from jax.experimental import pallas as pl
from jax.experimental.pallas import tpu as pltpu
from jax.sharding import PartitionSpec as P

GROUPS = 32
EPS = 1e-05
MESH = pl.DeviceIdType.MESH
BF = jnp.bfloat16
F32 = jnp.float32
R, C, CH = 20, 40, 640
BLK = 240
CUT = 128
STRIDE = 56
DELTAS = (0, 3, 1, 2)


def dot(a, b):
    return jnp.dot(a, b, preferred_element_type=F32)


def dot3(a, b):
    hi = a.astype(BF)
    rest = a - hi.astype(F32)
    mid = rest.astype(BF)
    low = (rest - mid.astype(F32)).astype(BF)
    return dot(hi, b) + dot(mid, b) + dot(low, b)


def kernel(
    feat, mask, gain, shift, weight, mask_w, bias, out,
    wall, wm, act, even, odd, acc, col_out, row_in, col_in, cor_in,
    mask_in, mpad, mcols, mtaps, gtab, st_out, st_in,
    z_s, z_r, f_s, f_r, fh_s, fh_r, l_s, l_r, lh_s, lh_r, c_s, c_r, h_s, h_r, t_s, t_r,
):
    dp, row, col = lax.axis_index("dp"), lax.axis_index("row"), lax.axis_index("col")
    x, core = row // 2, row % 2
    y, zh = dp // 4, dp % 4

    def at(y_, zh_, x_, core_, col_):
        return (y_ * 4 + zh_, x_ * 2 + core_, col_)

    up, down = (row + 7) % 8, (row + 1) % 8
    left, right = (col + 3) % 4, (col + 1) % 4
    group = [(dp, (row + i) % 8, (col + j) % 4) for i in range(8) for j in range(4) if i or j]
    far = [at(y, (zh + s) % 4, x, core, col) for s in (1, 3, 2)]
    xn = [at(y, zh, (x + 1) % 4, core, col), at(y, zh, (x + 3) % 4, core, col)]
    yn = [at((y + 1) % 4, zh, x, core, col), at((y + 3) % 4, zh, x, core, col)]
    first = core == 0
    fdev = [tuple(jnp.where(first, a, b) for a, b in zip(yn[i], xn[i])) for i in range(2)]
    ldev = [tuple(jnp.where(first, b, a) for a, b in zip(yn[i], xn[i])) for i in range(2)]
    sib = at(y, zh, x, 1 - core, col)
    fme = jnp.where(first, y, x)
    lme = jnp.where(first, x, y)
    zof = [(zh + d) % 4 for d in DELTAS]

    barrier = pltpu.get_barrier_semaphore()
    peers = far + yn + group
    for d in peers:
        pl.semaphore_signal(barrier, inc=1, device_id=d, device_id_type=MESH)

    isodd = zh % 2 == 1
    zero8 = jnp.zeros((8, CH), F32)

    def both(a, b):
        return jnp.where(isodd, b, a)

    def pair(j):
        s, t = weight[2 * j].astype(F32), weight[2 * j + 1].astype(F32)
        a = jnp.concatenate([s, t[32:40], t[0:32]], axis=0)
        b = jnp.concatenate([s[8:40], t[0:8], s[0:8], t[8:40]], axis=0)
        return both(a, b).astype(BF)

    @pl.when(first)
    def _():
        v = pair(x)
        for n in range(3):
            wall[0, zh, x, y, 80 * n : 80 * n + 80, :] = v[:, 128 * n : 128 * n + 128]

    @pl.when(jnp.logical_not(first))
    def _():
        last = weight[8].astype(F32)
        tail = both(
            jnp.concatenate([last, zero8], axis=0), jnp.concatenate([zero8, last], axis=0)
        ).astype(BF)
        for j in range(4):
            v = pair(j)
            for n in range(2):
                wall[1, zh, y, j, 80 * n : 80 * n + 80, :] = v[:, 384 + 128 * n : 512 + 128 * n]
            for s in range(4):
                m = 4 * j + s
                if m < 15:
                    n, r = m // 3, m % 3
                    wall[1, zh, y, j, 160 + 16 * s : 176 + 16 * s, :] = tail[
                        16 * r : 16 * r + 16, 128 * n : 128 * n + 128
                    ]
                else:
                    wall[1, zh, y, j, 160 + 16 * s : 176 + 16 * s, :] = jnp.zeros((16, 128), BF)
            wall[1, zh, y, j, 224:240, :] = jnp.zeros((16, 128), BF)

    def pass1(r, total):
        v = feat[r].astype(F32)
        col_out[0, pl.ds(r, 1), :] = v[0:1]
        col_out[1, pl.ds(r, 1), :] = v[39:40]
        return total + v[0:8] + v[8:16] + v[16:24] + v[24:32] + v[32:40]

    zeros = jnp.zeros((8, CH), F32)
    col_out[0, 16:24, :] = zeros
    col_out[1, 16:24, :] = zeros
    total = lax.fori_loop(0, R, pass1, zeros)

    pl.semaphore_wait(barrier, len(peers))

    def copy(src, dst, s, r, d):
        return pltpu.make_async_remote_copy(src, dst, s, r, device_id=d, device_id_type=MESH)

    def zc(i):
        blk = wall.at[core, zh, lme, fme]
        return copy(blk, blk, z_s.at[i], z_r.at[i], far[i])

    def zin(k):
        i = {3: 0, 1: 1, 2: 2}[DELTAS[k]]
        blk = wall.at[core, zof[k], lme, fme]
        return copy(blk, blk, z_s.at[i], z_r.at[i], far[i])

    def fc(k, i, who):
        blk = wall.at[core, zof[k], lme, (fme + who) % 4]
        return copy(blk, blk, f_s.at[k, i], f_r.at[k, i], fdev[i])

    def fhc(k, i, who):
        rows = pl.ds(0, CUT) if i == 0 else pl.ds(CUT, BLK - CUT)
        blk = wall.at[core, zof[k], lme, (fme + who) % 4, rows]
        return copy(blk, blk, fh_s.at[k, i], fh_r.at[k, i], fdev[i])

    def lc(k, i, who):
        blk = wall.at[core, zof[k], (lme + who) % 4]
        return copy(blk, blk, l_s.at[k, i], l_r.at[k, i], ldev[i])

    def lhc(k, i, who):
        blk = wall.at[core, zof[k], (lme + who) % 4, pl.ds(2 * i, 2)]
        return copy(blk, blk, lh_s.at[k, i], lh_r.at[k, i], ldev[i])

    def sc(k, which):
        blk = wall.at[which, zof[k]]
        return copy(blk, blk, c_s.at[k], c_r.at[k], sib)

    def f_send(k):
        fc(k, 0, 0).start()
        fc(k, 1, 0).start()

    def f_fwd(k):
        fc(k, 0, 3).wait_recv()
        fhc(k, 0, 3).start()
        fc(k, 1, 1).wait_recv()
        fhc(k, 1, 1).start()

    def f_done(k):
        fhc(k, 0, 2).wait_recv()
        fhc(k, 1, 2).wait_recv()

    def f_sent(k):
        fc(k, 0, 0).wait_send()
        fc(k, 1, 0).wait_send()
        fhc(k, 0, 3).wait_send()
        fhc(k, 1, 1).wait_send()

    def l_send(k):
        lc(k, 0, 0).start()
        lc(k, 1, 0).start()

    def l_fwd(k):
        lc(k, 0, 3).wait_recv()
        lhc(k, 0, 3).start()
        lc(k, 1, 1).wait_recv()
        lhc(k, 1, 1).start()

    def l_done(k):
        lhc(k, 0, 2).wait_recv()
        lhc(k, 1, 2).wait_recv()

    def l_sent(k):
        lc(k, 0, 0).wait_send()
        lc(k, 1, 0).wait_send()
        lhc(k, 0, 3).wait_send()
        lhc(k, 1, 1).wait_send()

    for i in range(3):
        zc(i).start()

    @pl.when(first)
    def _():
        f_send(0)

    @pl.when(jnp.logical_not(first))
    def _():
        l_send(0)

    halo = [
        (feat.at[R - 1], row_in.at[0], (dp, down, col)),
        (feat.at[0], row_in.at[1], (dp, up, col)),
        (col_out.at[1], col_in.at[0], (dp, row, right)),
        (col_out.at[0], col_in.at[1], (dp, row, left)),
        (col_out.at[1, pl.ds(16, 8)], cor_in.at[0], (dp, down, right)),
        (col_out.at[0, pl.ds(16, 8)], cor_in.at[1], (dp, down, left)),
        (col_out.at[1, pl.ds(0, 8)], cor_in.at[2], (dp, up, right)),
        (col_out.at[0, pl.ds(0, 8)], cor_in.at[3], (dp, up, left)),
    ]
    around = [
        (dp, down, right), (dp, down, col), (dp, down, left),
        (dp, row, right), (dp, row, left),
        (dp, up, right), (dp, up, col), (dp, up, left),
    ]
    halo += [(mask, mask_in.at[i], d) for i, d in enumerate(around)]
    hcs = [copy(s, d, h_s.at[i], h_r.at[i], dev) for i, (s, d, dev) in enumerate(halo)]
    for c in hcs:
        c.start()

    chan = lax.broadcasted_iota(jnp.int32, (CH, 128), 0)
    lane = lax.broadcasted_iota(jnp.int32, (CH, 128), 1)
    per = CH // GROUPS
    gm = jnp.where((chan >= lane * per) & (chan < lane * per + per), 1.0, 0.0).astype(BF)
    lane_t = lax.broadcasted_iota(jnp.int32, (128, CH), 0)
    chan_t = lax.broadcasted_iota(jnp.int32, (128, CH), 1)
    gt = jnp.where((chan_t >= lane_t * per) & (chan_t < lane_t * per + per), 1.0, 0.0).astype(BF)

    def spread(v):
        return jnp.broadcast_to(jnp.sum(v, axis=0, keepdims=True), v.shape)

    n_here = float(R * C * per)
    mean_here = dot3(spread(total), gm) * (1.0 / n_here)
    mean_chan = dot3(mean_here, gt)[0:1]

    def pass2(r, total):
        d = feat[r].astype(F32) - mean_chan
        d = d * d
        return total + d[0:8] + d[8:16] + d[16:24] + d[24:32] + d[32:40]

    m2 = dot3(spread(lax.fori_loop(0, R, pass2, zeros)), gm)
    sub = lax.broadcasted_iota(jnp.int32, (8, 128), 0)
    st_out[...] = jnp.where(sub == 0, mean_here, m2)
    tcs = [copy(st_out, st_in.at[i], t_s.at[i], t_r.at[i], d) for i, d in enumerate(group)]
    for c in tcs:
        c.start()

    @pl.when(first)
    def _():
        f_fwd(0)
        f_done(0)
        l_send(0)

    zin(1).wait_recv()
    f_send(1)
    zin(2).wait_recv()
    f_send(2)

    for c in hcs[8:]:
        c.wait_recv()

    lane1 = lax.broadcasted_iota(jnp.int32, (R, 128), 1)

    def wide(v):
        return jnp.concatenate([v.astype(F32), jnp.zeros((R, 128 - C), F32)], axis=1)

    def strip(lef, mid, rig):
        a = pltpu.roll(wide(lef), 128 - 39, 1)
        b = pltpu.roll(wide(mid), 1, 1)
        c = pltpu.roll(wide(rig), 41, 1)
        res = jnp.where((lane1 >= 1) & (lane1 <= 40), b, 0.0)
        res = jnp.where((lane1 == 0) & (col > 0), a, res)
        return jnp.where((lane1 == 41) & (col < 3), c, res)

    above = strip(mask_in[0], mask_in[1], mask_in[2])
    here = strip(mask_in[3], mask[...], mask_in[4])
    below = strip(mask_in[5], mask_in[6], mask_in[7])
    mpad[...] = jnp.zeros((128, 128), F32)
    mpad[0:1, :] = jnp.where(row > 0, above[19:20], 0.0)
    mpad[1:21, :] = here
    mpad[21:22, :] = jnp.where(row < 7, below[0:1], 0.0)
    mcols[...] = mpad[...].T
    d3 = mcols[0:40, :] + pltpu.roll(mcols[1:41, :], 32, 1) + pltpu.roll(mcols[2:42, :], 64, 1)

    def fill_mask(p, _):
        a = pltpu.roll(d3, lax.rem(128 - 2 * p, 128), 1)
        b = pltpu.roll(d3, lax.rem(127 - 2 * p, 128), 1)
        mtaps[pl.ds(pl.multiple_of(80 * p, 80), 80), :] = jnp.concatenate([a, b], axis=0).astype(BF)
        return 0

    lax.fori_loop(0, 10, fill_mask, 0)
    gtab[...] = jnp.zeros((128, CH), F32)
    for dy in range(3):
        for dx in range(3):
            gtab[32 * dx + dy : 32 * dx + dy + 1, :] = mask_w[3 * dy + dx : 3 * dy + dx + 1, :]
    g = gtab[...]
    g_hi = g.astype(BF)
    g_rest = g - g_hi.astype(F32)
    g_mid = g_rest.astype(BF)
    g_low = (g_rest - g_mid.astype(F32)).astype(BF)
    bias_row = bias[...]

    def mask_term(p, _):
        rows = pl.ds(pl.multiple_of(80 * p, 80), 80)
        m = mtaps[rows, :]
        acc[rows, :] = dot(m, g_hi) + dot(m, g_mid) + dot(m, g_low) + bias_row
        return 0

    lax.fori_loop(0, 10, mask_term, 0)

    f_fwd(1)
    f_fwd(2)

    for c in tcs:
        c.wait_recv()
    means = st_out[0:1, :]
    for i in range(31):
        means = means + st_in[i, 0:1, :]
    mean_g = means * (1.0 / 32.0)
    dm = st_out[0:1, :] - mean_g
    sq = st_out[1:2, :] + n_here * dm * dm
    for i in range(31):
        dm = st_in[i, 0:1, :] - mean_g
        sq = sq + st_in[i, 1:2, :] + n_here * dm * dm
    rs_g = lax.rsqrt(sq * (1.0 / (32.0 * n_here)) + EPS)
    both_g = dot3(jnp.concatenate([mean_g, rs_g, jnp.zeros((6, 128), F32)], axis=0), gt)
    mean_c, rs_c = both_g[0:1], both_g[1:2]
    gain_c, shift_c = gain[...], shift[...]

    def activate(v):
        v = (v - mean_c) * rs_c * gain_c + shift_c
        return v / (1.0 + jnp.exp(-v))

    f_done(1)
    l_send(1)
    f_done(2)
    l_send(2)

    def act_row(r, _):
        act[r + 1, 8 : 8 + C, :] = activate(feat[r].astype(F32))
        return 0

    lax.fori_loop(0, R, act_row, 0)
    for c in hcs[:8]:
        c.wait_recv()
    act[0, 8 : 8 + C, :] = jnp.where(row > 0, activate(row_in[0].astype(F32)), 0.0)
    act[21, 8 : 8 + C, :] = jnp.where(
        row < 7, activate(row_in[1].astype(F32)), 0.0
    )
    for side, there, off in ((0, col > 0, 7), (1, col < 3, 48)):
        edge = jnp.where(there, activate(col_in[side]), 0.0)
        for r in range(R):
            act[r + 1, off : off + 1, :] = edge[r : r + 1]
    for i, (there, pick, r, spot) in enumerate((
        ((row > 0) & (col > 0), 3, 0, 7),
        ((row > 0) & (col < 3), 3, 0, 48),
        ((row < 7) & (col > 0), 0, 21, 7),
        ((row < 7) & (col < 3), 0, 21, 48),
    )):
        corner = jnp.where(there, activate(cor_in[i]), 0.0)
        act[r, spot : spot + 1, :] = corner[pick : pick + 1]

    l_fwd(0)
    zin(3).wait_recv()
    f_send(3)

    def taps(p, first_row):
        r = 2 * p + first_row
        res = []
        for dx in range(3):
            a = act[r, 7 + dx : 7 + dx + C, :]
            b = act[r + 1, 7 + dx : 7 + dx + C, :]
            res.append(jnp.concatenate([a, b], axis=0).astype(BF))
        return res

    def fill_even(p, _):
        for dx, v in enumerate(taps(p, 0)):
            even[dx, pl.ds(pl.multiple_of(80 * p, 80), 80), :] = v
        return 0

    def fill_odd(p, _):
        for dx, v in enumerate(taps(p, 1)):
            odd[dx, pl.ds(pl.multiple_of(80 * p, 80), 80), :] = v
        return 0

    lax.fori_loop(0, 11, fill_even, 0)
    l_done(0)
    sc(0, core).start()
    l_fwd(1)
    f_fwd(3)
    lax.fori_loop(0, 10, fill_odd, 0)
    l_fwd(2)
    f_done(3)
    l_send(3)
    l_done(1)
    sc(1, core).start()
    l_done(2)
    sc(2, core).start()
    l_fwd(3)
    l_done(3)
    sc(3, core).start()
    for k in range(4):
        sc(k, 1 - core).wait_recv()

    low_half = lax.broadcasted_iota(jnp.int32, (16, 128), 0) < 8

    def merge(i, _):
        yy, zz = i // 2, 2 * (i % 2)
        base = pl.multiple_of((4 * yy + zz) * 40, 80)
        for j in range(4):
            for n in range(5):
                if n < 3:
                    a = wall.at[0, zz, j, yy, pl.ds(80 * n, 80)]
                    b = wall.at[0, zz + 1, j, yy, pl.ds(80 * n, 80)]
                else:
                    a = wall.at[1, zz, yy, j, pl.ds(80 * (n - 3), 80)]
                    b = wall.at[1, zz + 1, yy, j, pl.ds(80 * (n - 3), 80)]
                a2, b2 = a[32:48, :].astype(F32), b[32:48, :].astype(F32)
                mid_s = jnp.where(low_half, a2, b2).astype(BF)
                mid_t = jnp.concatenate([a2[8:16], b2[0:8]], axis=0).astype(BF)
                ln = pl.ds(128 * n, 128)
                wm[2 * j, pl.ds(base, 80), ln] = jnp.concatenate(
                    [a[0:32, :], mid_s, b[0:32, :]], axis=0
                )
                wm[2 * j + 1, pl.ds(base, 80), ln] = jnp.concatenate(
                    [a[48:80, :], mid_t, b[48:80, :]], axis=0
                )
        for n in range(5):
            def tile(z_, r):
                m = 3 * n + r
                return wall[1, z_, yy, m // 4, pl.ds(160 + 16 * (m % 4), 16), :]
            mid = jnp.where(low_half, tile(zz, 2).astype(F32), tile(zz + 1, 0).astype(F32))
            wm[8, pl.ds(base, 80), pl.ds(128 * n, 128)] = jnp.concatenate(
                [tile(zz, 0), tile(zz, 1), mid.astype(BF), tile(zz + 1, 1), tile(zz + 1, 2)], axis=0
            )
        return 0

    lax.fori_loop(0, 8, merge, 0)

    for dy in range(3):
        def conv(dx, _):
            lhs = odd[dx] if dy == 1 else even[dx, pl.ds(40 * dy, 800), :]
            acc[...] += dot(lhs, wm[3 * dy + dx])
            return 0

        lax.fori_loop(0, 3, conv, 0)
    out[...] = acc[...].astype(BF)

    for i in range(3):
        zc(i).wait_send()

    @pl.when(first)
    def _():
        f_sent(0)

    for k in range(1, 4):
        f_sent(k)
    for k in range(4):
        l_sent(k)
        sc(k, core).wait_send()
    for c in hcs + tcs:
        c.wait_send()


def local(features, hole_mask, norm_gain, norm_shift, conv_weight, mask_weight, conv_bias):
    vm = pl.BlockSpec(memory_space=pltpu.VMEM)
    dma = pltpu.SemaphoreType.DMA
    result = pl.pallas_call(
        kernel,
        out_shape=jax.ShapeDtypeStruct((R * C, CH), BF),
        in_specs=[vm] * 7,
        out_specs=vm,
        scratch_shapes=[
            pltpu.VMEM((2, 4, 4, 4, BLK, 128), BF),
            pltpu.VMEM((9, CH, CH), BF),
            pltpu.VMEM((22, STRIDE, CH), F32),
            pltpu.VMEM((3, 22 * C, CH), BF),
            pltpu.VMEM((3, R * C, CH), BF),
            pltpu.VMEM((R * C, CH), F32),
            pltpu.VMEM((2, 24, CH), F32),
            pltpu.VMEM((2, C, CH), BF),
            pltpu.VMEM((2, 24, CH), F32),
            pltpu.VMEM((4, 8, CH), F32),
            pltpu.VMEM((8, R, C), jnp.int32),
            pltpu.VMEM((128, 128), F32),
            pltpu.VMEM((128, 128), F32),
            pltpu.VMEM((R * C, 128), BF),
            pltpu.VMEM((128, CH), F32),
            pltpu.VMEM((8, 128), F32),
            pltpu.VMEM((31, 8, 128), F32),
            dma((3,)), dma((3,)),
            dma((4, 2)), dma((4, 2)), dma((4, 2)), dma((4, 2)),
            dma((4, 2)), dma((4, 2)), dma((4, 2)), dma((4, 2)),
            dma((4,)), dma((4,)), dma((16,)), dma((16,)), dma((31,)), dma((31,)),
        ],
        compiler_params=pltpu.CompilerParams(
            collective_id=0, has_side_effects=True, vmem_limit_bytes=56 << 20
        ),
        name="conv",
    )(
        features[0], hole_mask[0], norm_gain.reshape(1, CH), norm_shift.reshape(1, CH),
        conv_weight, mask_weight, conv_bias.reshape(1, CH),
    )
    return result.reshape(1, R, C, CH)


def solution(mesh):
    image = P("dp", "row", "col", None)
    return jax.shard_map(
        local,
        mesh=mesh,
        in_specs=(image, P("dp", "row", "col"), P(), P(), P(None, "dp", None), P(), P()),
        out_specs=image,
        check_vma=False,
    )
```

time: 282 us -> 89.9 us (0.32)
  the two profiles are of different devices: /device:TPU:145 before, /device:TPU:1 now
where the time goes in v1:
time: 89.9 us; the launch traced here: 89.7 us
  Pallas kernels  84.3 us (94%)
  local copies, waits for them, and re-layouts  5.34 us (6%)
    pallas_call x1, Pallas kernels, local(): pl.pallas_call(kernel, out_shape=jax.ShapeDtypeStruct((R * C, CH), BF), i...  84.3 us
    unnamed x8, local copies, waits for them, and re-layouts  2.87 us

profile of v1, /device:TPU:1, one launch (start us, length us, event | category | flops | bytes accessed | tf_op | source)
XLA Modules:
  0.0 89.7 jit_solution(5934211934674766335)
XLA Ops:
  0.0 0.0 copy-start.1
  0.0 0.0 copy-start.2
  0.0 0.0 copy-start
  0.0 1.3 %reshape.12.gain = f32[1,640]{1,0:T(1,128)} reshape(f32[640]{0:T(1024)} %param.9) | data formatting | bytes 5120 | tf_op jit(solution)/shard_map/reshape | solution.py:500
  1.3 0.0 copy-done.1
  1.3 0.6 reshape.13.shift
  1.9 0.0 copy-done.2
  1.9 0.6 reshape.14.bias
  2.5 0.0 copy-done
  2.5 0.6 copy.10
  3.1 84.3 %conv.1 = bf16[800,640]{1,0:T(8,128)(2,1)} custom-call(bf16[20,40,640]{2,1,0:T(8,128)(2,1)} %bitcast.6, s32[20,40]{1,0:T(8,128)} %bitcast.7, f32[1,640]{1,0:T(1,128)} %reshape.12.gain, f32[1,640]{1,0:T(1,128)} %reshape.13.shift, bf16[9,40,640]{2,1,0:T(8,128)(2,1)} %weight.1, f32[9,640]{1,0:T(8,128)} %mask_w.1, f32[1,640]{1,0:T(1,128)} %reshape.14.bias), custom_call_target="tpu_custom_call" | custom-call | tf_op jit(solution)/shard_map/conv/pallas_call | solution.py:467
  87.4 2.3 %copy.12 = bf16[1,20,40,640]{3,2,1,0:T(8,128)(2,1)} copy(bf16[1,20,40,640]{3,2,1,0:T(8,128)(2,1)} %bitcast.5) | data formatting | bytes 2048000
Async XLA Ops:
  0.0 1.3 %copy-start.1 = (f32[640]{0:T(1024)S(1)}, f32[640]{0:T(1024)}, u32[]{:S(2)}) copy-start(f32[640]{0:T(1024)} %param.10) | copy-start | bytes 7684
  0.0 1.9 %copy-start.2 = (f32[640]{0:T(1024)S(1)}, f32[640]{0:T(1024)}, u32[]{:S(2)}) copy-start(f32[640]{0:T(1024)} %param.13) | copy-start | bytes 7684
  0.0 2.5 %copy-start = (s32[1,20,40]{2,0,1:T(1,128)S(1)}, s32[1,20,40]{2,0,1:T(1,128)}, u32[]{:S(2)}) copy-start(s32[1,20,40]{2,0,1:T(1,128)} %param.8) | copy-start | bytes 9604

commit v2 on v1

v2 whole, which is shorter than its diff:
```python
import jax
import jax.numpy as jnp
from jax import lax
from jax.experimental import pallas as pl
from jax.experimental.pallas import tpu as pltpu
from jax.sharding import PartitionSpec as P

GROUPS = 32
EPS = 1e-05
MESH = pl.DeviceIdType.MESH
BF = jnp.bfloat16
F32 = jnp.float32
R, C, CH = 20, 40, 640
BLK = 240
CUT = 128
STRIDE = 56
DELTAS = (0, 3, 1, 2)


def dot(a, b):
    return jnp.dot(a, b, preferred_element_type=F32)


def dot3(a, b):
    hi = a.astype(BF)
    rest = a - hi.astype(F32)
    mid = rest.astype(BF)
    low = (rest - mid.astype(F32)).astype(BF)
    return dot(hi, b) + dot(mid, b) + dot(low, b)


def kernel(
    feat4, mask3, gain, shift, weight, mask_w, bias, out4,
    wall, wm, act, taps, acc, feat, col_out, row_in, col_in, cor_in,
    mask_in, mpad, mcols, mtaps, gtab, st_out, st_in,
    z_s, z_r, f_s, f_r, fh_s, fh_r, p_s, p_r, q_s, q_r, c_s, c_r, h_s, h_r, t_s, t_r, in_sem, feat_raw,
):
    mask = mask3.at[0]
    dp, row, col = lax.axis_index("dp"), lax.axis_index("row"), lax.axis_index("col")
    x, core = row // 2, row % 2
    y, zh = dp // 4, dp % 4

    def at(y_, zh_, x_, core_, col_):
        return (y_ * 4 + zh_, x_ * 2 + core_, col_)

    up, down = (row + 7) % 8, (row + 1) % 8
    left, right = (col + 3) % 4, (col + 1) % 4
    far = [at(y, (zh + s) % 4, x, core, col) for s in (1, 3, 2)]
    xn = [at(y, zh, (x + 1) % 4, core, col), at(y, zh, (x + 3) % 4, core, col)]
    yn = [at((y + 1) % 4, zh, x, core, col), at((y + 3) % 4, zh, x, core, col)]
    first = core == 0
    fdev = [tuple(jnp.where(first, a, b) for a, b in zip(yn[i], xn[i])) for i in range(2)]
    ldev = [tuple(jnp.where(first, b, a) for a, b in zip(yn[i], xn[i])) for i in range(2)]
    sib = at(y, zh, x, 1 - core, col)
    fme = jnp.where(first, y, x)
    lme = jnp.where(first, x, y)
    zof = [(zh + d) % 4 for d in DELTAS]

    feat_in = pltpu.make_async_copy(feat4.at[0], feat_raw, in_sem)
    feat_in.start()
    barrier = pltpu.get_barrier_semaphore()
    for d in far + yn:
        pl.semaphore_signal(barrier, inc=1, device_id=d, device_id_type=MESH)

    def peer(t):
        return (dp, (row + t // 4) % 8, (col + t % 4) % 4)

    def greet(t, _):
        pl.semaphore_signal(barrier, inc=1, device_id=peer(t), device_id_type=MESH)
        return 0

    lax.fori_loop(1, 32, greet, 0)

    isodd = y % 2 == 1
    zero8 = jnp.zeros((8, CH), F32)

    def both(a, b):
        return jnp.where(isodd, b, a)

    def pair(j):
        s, t = weight[2 * j].astype(F32), weight[2 * j + 1].astype(F32)
        a = jnp.concatenate([s, t[32:40], t[0:32]], axis=0)
        b = jnp.concatenate([s[8:40], t[0:8], s[0:8], t[8:40]], axis=0)
        return both(a, b).astype(BF)

    @pl.when(first)
    def _():
        for j in range(4):
            v = pair(j)
            for n in range(3):
                wall[0, zh, j, y, 80 * n : 80 * n + 80, :] = v[:, 128 * n : 128 * n + 128]

    @pl.when(jnp.logical_not(first))
    def _():
        last = weight[8].astype(F32)
        tail = both(
            jnp.concatenate([last, zero8], axis=0), jnp.concatenate([zero8, last], axis=0)
        ).astype(BF)
        for j in range(4):
            v = pair(j)
            for n in range(2):
                wall[1, zh, y, j, 80 * n : 80 * n + 80, :] = v[:, 384 + 128 * n : 512 + 128 * n]
            for s in range(4):
                m = 4 * j + s
                if m < 15:
                    n, r = m // 3, m % 3
                    wall[1, zh, y, j, 160 + 16 * s : 176 + 16 * s, :] = tail[
                        16 * r : 16 * r + 16, 128 * n : 128 * n + 128
                    ]
                else:
                    wall[1, zh, y, j, 160 + 16 * s : 176 + 16 * s, :] = jnp.zeros((16, 128), BF)
            wall[1, zh, y, j, 224:240, :] = jnp.zeros((16, 128), BF)

    def clear(t, _):
        for k in range(4):
            wm[k, t] = jnp.zeros((256, CH), BF)
        return 0

    lax.fori_loop(0, 9, clear, 0)
    pl.semaphore_wait(barrier, 36)

    def copy(src, dst, s, r, d):
        return pltpu.make_async_remote_copy(src, dst, s, r, device_id=d, device_id_type=MESH)

    def zc(i):
        blk = wall.at[core, zh, lme, fme]
        return copy(blk, blk, z_s.at[i], z_r.at[i], far[i])

    def zin(k):
        i = {3: 0, 1: 1, 2: 2}[DELTAS[k]]
        blk = wall.at[core, zof[k], lme, fme]
        return copy(blk, blk, z_s.at[i], z_r.at[i], far[i])

    def fc(k, i, who):
        blk = wall.at[core, zof[k], lme, (fme + who) % 4]
        return copy(blk, blk, f_s.at[k, i], f_r.at[k, i], fdev[i])

    def fhc(k, i, who):
        rows = pl.ds(0, CUT) if i == 0 else pl.ds(CUT, BLK - CUT)
        blk = wall.at[core, zof[k], lme, (fme + who) % 4, rows]
        return copy(blk, blk, fh_s.at[k, i], fh_r.at[k, i], fdev[i])

    def pc(k, e, i, who):
        blk = wall.at[core, zof[k], (lme + who) % 4, (fme + e) % 4]
        return copy(blk, blk, p_s.at[k, e, i], p_r.at[k, e, i], ldev[i])

    def qc(k, e, who):
        blk = wall.at[core, zof[k], (lme + who) % 4, (fme + e) % 4]
        return copy(blk, blk, q_s.at[k, e], q_r.at[k, e], ldev[0 if e < 2 else 1])

    def sc(k, w, which):
        l_there = jnp.where(core == which, lme, jnp.where(first, y, x))
        blk = wall.at[which, zof[k], (l_there + w) % 4]
        return copy(blk, blk, c_s.at[k, w], c_r.at[k, w], sib)

    def f_send(k):
        fc(k, 0, 0).start()
        fc(k, 1, 0).start()

    def f_fwd(k):
        fc(k, 0, 3).wait_recv()
        fhc(k, 0, 3).start()
        fc(k, 1, 1).wait_recv()
        fhc(k, 1, 1).start()

    def f_done(k):
        fhc(k, 0, 2).wait_recv()
        fhc(k, 1, 2).wait_recv()

    def f_sent(k):
        fc(k, 0, 0).wait_send()
        fc(k, 1, 0).wait_send()
        fhc(k, 0, 3).wait_send()
        fhc(k, 1, 1).wait_send()

    def on(k, e, cond_fn):
        if k == 0 and e == 0:
            pl.when(jnp.logical_not(first))(cond_fn)
        else:
            cond_fn()

    def l_send(k, e):
        pc(k, e, 0, 0).start()
        pc(k, e, 1, 0).start()

    def l_fwd(k, *es):
        for e in es:
            def go(e=e):
                i, who = (0, 3) if e < 2 else (1, 1)
                pc(k, e, i, who).wait_recv()
                qc(k, e, who).start()
            on(k, e, go)

    def l_other(k):
        for e in range(4):
            def go(e=e):
                i, who = (1, 1) if e < 2 else (0, 3)
                pc(k, e, i, who).wait_recv()
            on(k, e, go)

    def l_last(k):
        for e in range(4):
            on(k, e, lambda e=e: qc(k, e, 2).wait_recv())

    def l_sent(k):
        for e in range(4):
            def go(e=e):
                pc(k, e, 0, 0).wait_send()
                pc(k, e, 1, 0).wait_send()
                qc(k, e, 3 if e < 2 else 1).wait_send()
            on(k, e, go)

    def s_send(k, *ws):
        for w in ws:
            sc(k, w, core).start()

    def s_wait(k):
        for w in range(4):
            sc(k, w, 1 - core).wait_recv()

    NEAR = (1, 3)
    zc(0).start()
    zc(1).start()

    @pl.when(first)
    def _():
        f_send(0)

    @pl.when(jnp.logical_not(first))
    def _():
        for e in (0, 1, 3, 2):
            l_send(0, e)

    zc(2).start()

    old = lax.broadcasted_iota(jnp.int32, (CH, 128), 0)
    shift_by = jnp.zeros((CH, 128), jnp.int32)
    for i in range(16):
        j = (i % 4) * 4 + i // 4
        shift_by = jnp.where(old >= 40 * i, 40 * (j - i), shift_by)
    target = old + shift_by
    lane0 = lax.broadcasted_iota(jnp.int32, (CH, 128), 1)
    perm = jnp.concatenate(
        [jnp.where(target == lane0 + 128 * n, 1.0, 0.0).astype(BF) for n in range(5)], axis=1
    )

    feat_in.wait()

    def stage(p, _):
        r = 2 * p
        two = jnp.concatenate([feat_raw[r].astype(F32), feat_raw[r + 1].astype(F32)], axis=0)
        feat[p] = two.astype(BF)
        return 0

    lax.fori_loop(0, R // 2, stage, 0)
    def reorder(h, _):
        v = dot(feat[pl.ds(5 * h, 5)].reshape(400, CH), perm)
        acc[pl.ds(pl.multiple_of(400 * h, 400), 400), :] = v
        return 0

    lax.fori_loop(0, 2, reorder, 0)

    def pass1(p, total):
        r = 2 * p
        v = acc[pl.ds(pl.multiple_of(80 * p, 80), 80), :]
        feat[p] = v.astype(BF)
        col_out[0, pl.ds(r, 1), :] = v[0:1]
        col_out[1, pl.ds(r, 1), :] = v[39:40]
        col_out[0, pl.ds(r + 1, 1), :] = v[40:41]
        col_out[1, pl.ds(r + 1, 1), :] = v[79:80]
        for i in range(10):
            total = total + v[8 * i : 8 * i + 8]
        return total

    zeros = jnp.zeros((8, CH), F32)
    col_out[0, 16:24, :] = zeros
    col_out[1, 16:24, :] = zeros
    total = lax.fori_loop(0, R // 2, pass1, zeros)


    halo = [
        (feat.at[R // 2 - 1], row_in.at[0], (dp, down, col)),
        (feat.at[0], row_in.at[1], (dp, up, col)),
        (col_out.at[1], col_in.at[0], (dp, row, right)),
        (col_out.at[0], col_in.at[1], (dp, row, left)),
        (col_out.at[1, pl.ds(16, 8)], cor_in.at[0], (dp, down, right)),
        (col_out.at[0, pl.ds(16, 8)], cor_in.at[1], (dp, down, left)),
        (col_out.at[1, pl.ds(0, 8)], cor_in.at[2], (dp, up, right)),
        (col_out.at[0, pl.ds(0, 8)], cor_in.at[3], (dp, up, left)),
    ]
    around = [
        (dp, down, right), (dp, down, col), (dp, down, left),
        (dp, row, right), (dp, row, left),
        (dp, up, right), (dp, up, col), (dp, up, left),
    ]
    halo += [(mask, mask_in.at[i], d) for i, d in enumerate(around)]
    hcs = [copy(s, d, h_s.at[i], h_r.at[i], dev) for i, (s, d, dev) in enumerate(halo)]
    for c in hcs:
        c.start()

    chan = lax.broadcasted_iota(jnp.int32, (CH, 128), 0)
    lane = lax.broadcasted_iota(jnp.int32, (CH, 128), 1)
    per = CH // GROUPS
    gm = jnp.where((chan >= lane * per) & (chan < lane * per + per), 1.0, 0.0).astype(BF)
    gm = lax.dot_general(perm, gm, (((0,), (0,)), ((), ())), preferred_element_type=F32).astype(BF)
    lane_t = lax.broadcasted_iota(jnp.int32, (128, CH), 0)
    chan_t = lax.broadcasted_iota(jnp.int32, (128, CH), 1)
    gt = jnp.where((chan_t >= lane_t * per) & (chan_t < lane_t * per + per), 1.0, 0.0).astype(BF)
    gt = dot(gt, perm).astype(BF)

    def spread(v):
        return jnp.broadcast_to(jnp.sum(v, axis=0, keepdims=True), v.shape)

    n_here = float(R * C * per)
    mean_here = dot3(spread(total), gm) * (1.0 / n_here)
    mean_chan = dot3(mean_here, gt)[0:1]

    def pass2(p, total):
        d = feat[p].astype(F32) - mean_chan
        d = d * d
        for i in range(10):
            total = total + d[8 * i : 8 * i + 8]
        return total

    m2 = dot3(spread(lax.fori_loop(0, R // 2, pass2, zeros)), gm)
    sub = lax.broadcasted_iota(jnp.int32, (8, 128), 0)
    st_out[...] = jnp.where(sub == 0, mean_here, m2)

    def tc(t):
        return copy(st_out, st_in.at[t], t_s.at[t], t_r.at[t], peer(t))

    def st_send(t, _):
        tc(t).start()
        return 0

    lax.fori_loop(1, 32, st_send, 0)

    @pl.when(first)
    def _():
        f_fwd(0)
        l_send(0, 1)
        l_send(0, 3)
        f_done(0)
        l_send(0, 2)

    s_send(0, 0)
    l_fwd(0, 0)
    zin(1).wait_recv()
    l_send(1, 0)
    f_send(1)
    zin(2).wait_recv()
    l_send(2, 0)
    f_send(2)

    for c in hcs[8:]:
        c.wait_recv()

    lane1 = lax.broadcasted_iota(jnp.int32, (R, 128), 1)

    def wide(v):
        return jnp.concatenate([v.astype(F32), jnp.zeros((R, 128 - C), F32)], axis=1)

    def strip(lef, mid, rig):
        a = pltpu.roll(wide(lef), 128 - 39, 1)
        b = pltpu.roll(wide(mid), 1, 1)
        c = pltpu.roll(wide(rig), 41, 1)
        res = jnp.where((lane1 >= 1) & (lane1 <= 40), b, 0.0)
        res = jnp.where((lane1 == 0) & (col > 0), a, res)
        return jnp.where((lane1 == 41) & (col < 3), c, res)

    above = strip(mask_in[0], mask_in[1], mask_in[2])
    here = strip(mask_in[3], mask[...], mask_in[4])
    below = strip(mask_in[5], mask_in[6], mask_in[7])
    mpad[...] = jnp.zeros((128, 128), F32)
    mpad[0:1, :] = jnp.where(row > 0, above[19:20], 0.0)
    mpad[1:21, :] = here
    mpad[21:22, :] = jnp.where(row < 7, below[0:1], 0.0)
    mcols[...] = mpad[...].T
    d3 = mcols[0:40, :] + pltpu.roll(mcols[1:41, :], 32, 1) + pltpu.roll(mcols[2:42, :], 64, 1)

    def fill_mask(p, _):
        a = pltpu.roll(d3, lax.rem(128 - 2 * p, 128), 1)
        b = pltpu.roll(d3, lax.rem(127 - 2 * p, 128), 1)
        mtaps[pl.ds(pl.multiple_of(80 * p, 80), 80), :] = jnp.concatenate([a, b], axis=0).astype(BF)
        return 0

    lax.fori_loop(0, 10, fill_mask, 0)
    gtab[...] = jnp.zeros((128, CH), F32)
    for dy in range(3):
        for dx in range(3):
            gtab[32 * dx + dy : 32 * dx + dy + 1, :] = mask_w[3 * dy + dx : 3 * dy + dx + 1, :]
    g = gtab[...]
    g_hi = g.astype(BF)
    g_rest = g - g_hi.astype(F32)
    g_mid = g_rest.astype(BF)
    g_low = (g_rest - g_mid.astype(F32)).astype(BF)
    bias_row = bias[...].reshape(1, CH)

    g_all = jnp.concatenate([g_hi, g_mid, g_low], axis=0)

    def mask_term(h, _):
        rows = pl.ds(pl.multiple_of(400 * h, 400), 400)
        m = mtaps[rows, :]
        acc[rows, :] = dot(jnp.concatenate([m, m, m], axis=1), g_all) + bias_row
        return 0

    lax.fori_loop(0, 2, mask_term, 0)

    l_fwd(0, 1, 3, 2)
    f_fwd(1)
    l_send(1, 1)
    l_send(1, 3)
    f_fwd(2)
    l_send(2, 1)
    l_send(2, 3)

    def st_mean(t, total):
        tc(t).wait_recv()
        return total + st_in[t]

    mean_g = lax.fori_loop(1, 32, st_mean, st_out[...])[0:1] * (1.0 / 32.0)

    def st_sq(t, total):
        v = st_in[t]
        dm = v[0:1] - mean_g
        return total + v[1:2] + n_here * dm * dm

    dm = st_out[0:1, :] - mean_g
    sq = lax.fori_loop(1, 32, st_sq, st_out[1:2, :] + n_here * dm * dm)
    rs_g = lax.rsqrt(sq * (1.0 / (32.0 * n_here)) + EPS)
    both_g = dot3(jnp.concatenate([mean_g, rs_g, jnp.zeros((6, 128), F32)], axis=0), gt)
    mean_c, rs_c = both_g[0:1], both_g[1:2]
    gs = jnp.concatenate(
        [gain[...].reshape(1, CH), shift[...].reshape(1, CH), jnp.zeros((6, CH), F32)], axis=0
    )
    gs = dot3(gs, perm)
    gain_c, shift_c = gs[0:1], gs[1:2]

    def activate(v):
        v = (v - mean_c) * rs_c * gain_c + shift_c
        return v / (1.0 + jnp.exp(-v))

    f_done(1)
    l_send(1, 2)
    f_done(2)
    l_send(2, 2)
    l_fwd(1, 0)
    l_fwd(2, 0)
    s_send(1, 0)
    s_send(2, 0)
    l_other(0)
    s_send(0, 1, 3)

    def act_rows(p, _):
        v = activate(feat[p].astype(F32))
        act[2 * p + 1, 8 : 8 + C, :] = v[0:C]
        act[2 * p + 2, 8 : 8 + C, :] = v[C : 2 * C]
        return 0

    lax.fori_loop(0, 5, act_rows, 0)
    l_fwd(1, 1, 3)
    l_fwd(2, 1, 3)
    zin(3).wait_recv()
    l_send(3, 0)
    f_send(3)
    lax.fori_loop(5, 10, act_rows, 0)
    l_last(0)
    s_send(0, 2)
    f_fwd(3)
    l_send(3, 1)
    l_send(3, 3)
    l_fwd(1, 2)
    l_fwd(2, 2)

    for c in hcs[:8]:
        c.wait_recv()
    act[0, 8 : 8 + C, :] = jnp.where(row > 0, activate(row_in[0, 40:80].astype(F32)), 0.0)
    act[21, 8 : 8 + C, :] = jnp.where(row < 7, activate(row_in[1, 0:40].astype(F32)), 0.0)
    for side, there, off in ((0, col > 0, 7), (1, col < 3, 48)):
        edge = jnp.where(there, activate(col_in[side]), 0.0)
        for r in range(R):
            act[r + 1, off : off + 1, :] = edge[r : r + 1]
    for i, (there, pick, r, spot) in enumerate((
        ((row > 0) & (col > 0), 3, 0, 7),
        ((row > 0) & (col < 3), 3, 0, 48),
        ((row < 7) & (col > 0), 0, 21, 7),
        ((row < 7) & (col < 3), 0, 21, 48),
    )):
        corner = jnp.where(there, activate(cor_in[i]), 0.0)
        act[r, spot : spot + 1, :] = corner[pick : pick + 1]

    f_done(3)
    l_send(3, 2)
    s_send(3, 0)
    l_fwd(3, 0)

    def fill(p, _):
            r = jnp.where(p < 11, 2 * p, 2 * p - 21)
            for dx in range(3):
                a = act[r, 7 + dx : 7 + dx + C, :]
                b = act[r + 1, 7 + dx : 7 + dx + C, :]
                v = jnp.concatenate([a, b], axis=0).astype(BF)
                taps[dx, pl.ds(pl.multiple_of(80 * p, 80), 80), :] = v
            return 0

    lax.fori_loop(0, 11, fill, 0)
    l_other(1)
    s_send(1, 1, 3)
    l_other(2)
    s_send(2, 1, 3)
    lax.fori_loop(11, 21, fill, 0)
    l_fwd(3, 1, 3)

    low_half = lax.broadcasted_iota(jnp.int32, (16, 128), 0) < 8

    def delta(k):
        return jnp.where(k == 0, 0, jnp.where(k == 1, 3, jnp.where(k == 2, 1, 2)))

    def merge(k):
        z = lax.rem(zh + delta(k), 4)

        for m in range(2):
            base = pl.multiple_of(32 * z + 80 * m, 16)
            rows = pl.ds(base, 80)
            ya, yb = 2 * m, 2 * m + 1

            def two(j, _):
                for n in range(5):
                    if n < 3:
                        a = wall.at[0, z, j, ya, pl.ds(80 * n, 80)]
                        b = wall.at[0, z, j, yb, pl.ds(80 * n, 80)]
                    else:
                        a = wall.at[1, z, ya, j, pl.ds(80 * (n - 3), 80)]
                        b = wall.at[1, z, yb, j, pl.ds(80 * (n - 3), 80)]
                    a2, b2 = a[32:48, :].astype(F32), b[32:48, :].astype(F32)
                    mid_s = jnp.where(low_half, a2, b2).astype(BF)
                    mid_t = jnp.concatenate([a2[8:16], b2[0:8]], axis=0).astype(BF)
                    ln = pl.ds(128 * n, 128)
                    wm[k, 2 * j, rows, ln] = jnp.concatenate(
                        [a[0:32, :], mid_s, b[0:32, :]], axis=0
                    )
                    wm[k, 2 * j + 1, rows, ln] = jnp.concatenate(
                        [a[48:80, :], mid_t, b[48:80, :]], axis=0
                    )
                return 0

            lax.fori_loop(0, 4, two, 0)

            def tile(y_, n, r):
                i = 3 * n + r
                return wall[1, z, y_, i // 4, pl.ds(160 + 16 * (i % 4), 16), :]

            for n in range(5):
                mid = jnp.where(low_half, tile(ya, n, 2).astype(F32), tile(yb, n, 0).astype(F32))
                wm[k, 8, rows, pl.ds(128 * n, 128)] = jnp.concatenate(
                    [tile(ya, n, 0), tile(ya, n, 1), mid.astype(BF), tile(yb, n, 1), tile(yb, n, 2)],
                    axis=0,
                )

    def conv(k, dy):
        win = pl.ds(pl.multiple_of(128 * lax.rem(zh + delta(k), 4), 128), 256)
        start = pl.multiple_of(jnp.where(dy == 0, 0, jnp.where(dy == 1, 880, 80)), 80)
        parts = [taps[dx, pl.ds(start, R * C), win] for dx in range(3)]
        rhs = wm[k, pl.ds(3 * dy, 3)].reshape(768, CH)
        acc[...] += dot(jnp.concatenate(parts, axis=1), rhs)

    def step(t, _):
        k, dy = t // 3, lax.rem(t, 3)

        def when(there, *fs):
            @pl.when(t == there)
            def _():
                for f in fs:
                    f()

        for kk in range(4):
            when(3 * kk, lambda kk=kk: s_wait(kk))

        @pl.when(dy == 0)
        def _():
            merge(k)

        conv(k, dy)
        when(
            0,
            lambda: l_last(1), lambda: s_send(1, 2), lambda: l_last(2), lambda: s_send(2, 2),
            lambda: l_fwd(3, 2),
        )
        when(2, lambda: l_other(3), lambda: s_send(3, 1, 3))
        when(3, lambda: l_last(3), lambda: s_send(3, 2))
        return 0

    lax.fori_loop(0, 12, step, 0)
    def finish(r, _):
        out4[0, r] = acc[pl.ds(pl.multiple_of(C * r, 8), C), :].astype(BF)
        return 0

    lax.fori_loop(0, R, finish, 0)

    for i in range(3):
        zc(i).wait_send()

    @pl.when(first)
    def _():
        f_sent(0)

    for k in range(1, 4):
        f_sent(k)
    for k in range(4):
        l_sent(k)
        for w in range(4):
            sc(k, w, core).wait_send()
    for c in hcs:
        c.wait_send()

    def st_sent(t, _):
        tc(t).wait_send()
        return 0

    lax.fori_loop(1, 32, st_sent, 0)


def local(features, hole_mask, norm_gain, norm_shift, conv_weight, mask_weight, conv_bias):
    vm = pl.BlockSpec(memory_space=pltpu.VMEM)
    dma = pltpu.SemaphoreType.DMA
    result = pl.pallas_call(
        kernel,
        out_shape=jax.ShapeDtypeStruct((1, R, C, CH), BF),
        in_specs=[pl.BlockSpec(memory_space=pl.ANY)] + [vm] * 6,
        out_specs=vm,
        scratch_shapes=[
            pltpu.VMEM((2, 4, 4, 4, BLK, 128), BF),
            pltpu.VMEM((4, 9, 256, CH), BF),
            pltpu.VMEM((22, STRIDE, CH), F32),
            pltpu.VMEM((3, 42 * C, CH), BF),
            pltpu.VMEM((R * C, CH), F32),
            pltpu.VMEM((R // 2, 2 * C, CH), BF),
            pltpu.VMEM((2, 24, CH), F32),
            pltpu.VMEM((2, 2 * C, CH), BF),
            pltpu.VMEM((2, 24, CH), F32),
            pltpu.VMEM((4, 8, CH), F32),
            pltpu.VMEM((8, R, C), jnp.int32),
            pltpu.VMEM((128, 128), F32),
            pltpu.VMEM((128, 128), F32),
            pltpu.VMEM((R * C, 128), BF),
            pltpu.VMEM((128, CH), F32),
            pltpu.VMEM((8, 128), F32),
            pltpu.VMEM((32, 8, 128), F32),
            dma((3,)), dma((3,)),
            dma((4, 2)), dma((4, 2)), dma((4, 2)), dma((4, 2)),
            dma((4, 4, 2)), dma((4, 4, 2)), dma((4, 4)), dma((4, 4)),
            dma((4, 4)), dma((4, 4)), dma((16,)), dma((16,)), dma((32,)), dma((32,)), dma(()),
            pltpu.VMEM((R, C, CH), BF),
        ],
        compiler_params=pltpu.CompilerParams(
            collective_id=0, has_side_effects=True, vmem_limit_bytes=56 << 20
        ),
        name="conv",
    )(features, hole_mask, norm_gain, norm_shift, conv_weight, mask_weight, conv_bias)
    return result


def solution(mesh):
    image = P("dp", "row", "col", None)
    return jax.shard_map(
        local,
        mesh=mesh,
        in_specs=(image, P("dp", "row", "col"), P(), P(), P(None, "dp", None), P(), P()),
        out_specs=image,
        check_vma=False,
    )
```

time: 89.9 us -> 78.4 us (0.87)
  Pallas kernels: 84.3 us -> 74.4 us
  local copies, waits for them, and re-layouts: 5.34 us -> 3.56 us
    pallas_call x1, Pallas kernels: 84.3 us -> 74.4 us  [local(): pl.pallas_call(kernel, out_shape=jax.ShapeDtypeStruct((1, R, C, CH), BF),...]
    reshape x3 -> x0, local copies, waits for them, and re-layouts: 2.47 us -> none  [the longest x1 1.3 us: local(): norm_gain.reshape(1, CH)]
    unnamed x8 -> x2, local copies, waits for them, and re-layouts: 2.87 us -> 3.56 us
where the time goes in v2:
time: 78.4 us; the launch traced here: 78 us
  Pallas kernels  74.4 us (95%)
  local copies, waits for them, and re-layouts  3.56 us (5%)
    pallas_call x1, Pallas kernels, local(): pl.pallas_call(kernel, out_shape=jax.ShapeDtypeStruct((1, R, C, CH), BF),...  74.4 us
    unnamed x2, local copies, waits for them, and re-layouts  3.56 us

profile of v2, /device:TPU:1, one launch (start us, length us, event | category | flops | bytes accessed | tf_op | source)
XLA Modules:
  0.0 78.0 jit_solution(5753281559602300412)
XLA Ops:
  0.0 1.3 %copy.8.mask3 = s32[1,20,40]{2,1,0:T(8,128)} copy(s32[1,20,40]{2,0,1:T(1,128)} %param.8) | data formatting | bytes 6400 | tf_op args[1]
  1.3 74.4 %conv.1 = bf16[1,20,40,640]{3,2,1,0:T(8,128)(2,1)} custom-call(bf16[1,20,40,640]{3,2,1,0:T(8,128)(2,1)} %feat4.1, s32[1,20,40]{2,1,0:T(8,128)} %copy.8.mask3, f32[640]{0:T(1024)} %gain.1, f32[640]{0:T(1024)} %shift.1, bf16[9,40,640]{2,1,0:T(8,128)(2,1)} %weight.1, f32[9,640]{1,0:T(8,128)} %mask_w.1, f32[640]{0:T(1024)} %bias.1), custom_call_target="tpu_custom_call" | custom-call | tf_op jit(solution)/shard_map/conv/pallas_call | solution.py:626
  75.7 2.3 %copy.10 = bf16[1,20,40,640]{3,2,1,0:T(8,128)(2,1)} copy(bf16[1,20,40,640]{3,2,1,0:T(8,128)(2,1)} %conv.1) | data formatting | bytes 2048000

commit v3 on v2

--- a/solution.py
+++ b/solution.py
@@ -31,11 +31,10 @@
 
 def kernel(
     feat4, mask3, gain, shift, weight, mask_w, bias, out4,
-    wall, wm, act, taps, acc, feat, col_out, row_in, col_in, cor_in,
+    wall, wm, act, taps, acc, mask, feat, col_out, row_in, col_in, cor_in,
     mask_in, mpad, mcols, mtaps, gtab, st_out, st_in,
-    z_s, z_r, f_s, f_r, fh_s, fh_r, p_s, p_r, q_s, q_r, c_s, c_r, h_s, h_r, t_s, t_r, in_sem, feat_raw,
+    w_s, z_r, f_r, fh_r, p_r, q_r, c_r, h_s, h_r, m_r, t_s, t_r, in_sem, feat_raw,
 ):
-    mask = mask3.at[0]
     dp, row, col = lax.axis_index("dp"), lax.axis_index("row"), lax.axis_index("col")
     x, core = row // 2, row % 2
     y, zh = dp // 4, dp % 4
@@ -70,6 +69,9 @@
         return 0
 
     lax.fori_loop(1, 32, greet, 0)
+
+    for r in range(R):
+        mask[r : r + 1, :] = mask3[r]
 
     isodd = y % 2 == 1
     zero8 = jnp.zeros((8, CH), F32)
@@ -124,34 +126,34 @@
 
     def zc(i):
         blk = wall.at[core, zh, lme, fme]
-        return copy(blk, blk, z_s.at[i], z_r.at[i], far[i])
+        return copy(blk, blk, w_s, z_r.at[i], far[i])
 
     def zin(k):
         i = {3: 0, 1: 1, 2: 2}[DELTAS[k]]
         blk = wall.at[core, zof[k], lme, fme]
-        return copy(blk, blk, z_s.at[i], z_r.at[i], far[i])
+        return copy(blk, blk, w_s, z_r.at[i], far[i])
 
     def fc(k, i, who):
         blk = wall.at[core, zof[k], lme, (fme + who) % 4]
-        return copy(blk, blk, f_s.at[k, i], f_r.at[k, i], fdev[i])
+        return copy(blk, blk, w_s, f_r.at[k, i], fdev[i])
 
     def fhc(k, i, who):
         rows = pl.ds(0, CUT) if i == 0 else pl.ds(CUT, BLK - CUT)
         blk = wall.at[core, zof[k], lme, (fme + who) % 4, rows]
-        return copy(blk, blk, fh_s.at[k, i], fh_r.at[k, i], fdev[i])
+        return copy(blk, blk, w_s, fh_r.at[k, i], fdev[i])
 
     def pc(k, e, i, who):
         blk = wall.at[core, zof[k], (lme + who) % 4, (fme + e) % 4]
-        return copy(blk, blk, p_s.at[k, e, i], p_r.at[k, e, i], ldev[i])
+        return copy(blk, blk, w_s, p_r.at[k, e, i], ldev[i])
 
     def qc(k, e, who):
         blk = wall.at[core, zof[k], (lme + who) % 4, (fme + e) % 4]
-        return copy(blk, blk, q_s.at[k, e], q_r.at[k, e], ldev[0 if e < 2 else 1])
+        return copy(blk, blk, w_s, q_r.at[k, e], ldev[0 if e < 2 else 1])
 
     def sc(k, w, which):
         l_there = jnp.where(core == which, lme, jnp.where(first, y, x))
         blk = wall.at[which, zof[k], (l_there + w) % 4]
-        return copy(blk, blk, c_s.at[k, w], c_r.at[k, w], sib)
+        return copy(blk, blk, w_s, c_r.at[k], sib)
 
     def f_send(k):
         fc(k, 0, 0).start()
@@ -166,12 +168,6 @@
     def f_done(k):
         fhc(k, 0, 2).wait_recv()
         fhc(k, 1, 2).wait_recv()
-
-    def f_sent(k):
-        fc(k, 0, 0).wait_send()
-        fc(k, 1, 0).wait_send()
-        fhc(k, 0, 3).wait_send()
-        fhc(k, 1, 1).wait_send()
 
     def on(k, e, cond_fn):
         if k == 0 and e == 0:
@@ -202,23 +198,14 @@
         for e in range(4):
             on(k, e, lambda e=e: qc(k, e, 2).wait_recv())
 
-    def l_sent(k):
-        for e in range(4):
-            def go(e=e):
-                pc(k, e, 0, 0).wait_send()
-                pc(k, e, 1, 0).wait_send()
-                qc(k, e, 3 if e < 2 else 1).wait_send()
-            on(k, e, go)
-
     def s_send(k, *ws):
         for w in ws:
             sc(k, w, core).start()
 
     def s_wait(k):
-        for w in range(4):
-            sc(k, w, 1 - core).wait_recv()
-
-    NEAR = (1, 3)
+        blk = wall.at[1 - core, zof[k]]
+        copy(blk, blk, w_s, c_r.at[k], sib).wait_recv()
+
     zc(0).start()
     zc(1).start()
 
@@ -259,6 +246,14 @@
         return 0
 
     lax.fori_loop(0, 2, reorder, 0)
+
+    @pl.when(first)
+    def _():
+        f_fwd(0)
+        l_send(0, 1)
+        l_send(0, 3)
+
+    l_fwd(0, 0)
 
     def pass1(p, total):
         r = 2 * p
@@ -276,6 +271,13 @@
     col_out[0, 16:24, :] = zeros
     col_out[1, 16:24, :] = zeros
     total = lax.fori_loop(0, R // 2, pass1, zeros)
+
+    @pl.when(first)
+    def _():
+        f_done(0)
+        l_send(0, 2)
+
+    s_send(0, 0)
 
 
     halo = [
@@ -294,7 +296,10 @@
         (dp, up, right), (dp, up, col), (dp, up, left),
     ]
     halo += [(mask, mask_in.at[i], d) for i, d in enumerate(around)]
-    hcs = [copy(s, d, h_s.at[i], h_r.at[i], dev) for i, (s, d, dev) in enumerate(halo)]
+    hcs = [
+        copy(s, d, h_s.at[i], h_r.at[i] if i < 8 else m_r, dev)
+        for i, (s, d, dev) in enumerate(halo)
+    ]
     for c in hcs:
         c.start()
 
@@ -327,7 +332,7 @@
     st_out[...] = jnp.where(sub == 0, mean_here, m2)
 
     def tc(t):
-        return copy(st_out, st_in.at[t], t_s.at[t], t_r.at[t], peer(t))
+        return copy(st_out, st_in.at[t], t_s, t_r, peer(t))
 
     def st_send(t, _):
         tc(t).start()
@@ -335,25 +340,15 @@
 
     lax.fori_loop(1, 32, st_send, 0)
 
-    @pl.when(first)
-    def _():
-        f_fwd(0)
-        l_send(0, 1)
-        l_send(0, 3)
-        f_done(0)
-        l_send(0, 2)
-
-    s_send(0, 0)
-    l_fwd(0, 0)
     zin(1).wait_recv()
     l_send(1, 0)
     f_send(1)
     zin(2).wait_recv()
     l_send(2, 0)
     f_send(2)
-
-    for c in hcs[8:]:
-        c.wait_recv()
+    l_fwd(0, 1, 3)
+
+    copy(mask_in, mask_in, h_s.at[0], m_r, sib).wait_recv()
 
     lane1 = lax.broadcasted_iota(jnp.int32, (R, 128), 1)
 
@@ -406,16 +401,19 @@
 
     lax.fori_loop(0, 2, mask_term, 0)
 
-    l_fwd(0, 1, 3, 2)
     f_fwd(1)
     l_send(1, 1)
     l_send(1, 3)
     f_fwd(2)
     l_send(2, 1)
     l_send(2, 3)
+    l_fwd(0, 2)
+    l_fwd(1, 0)
+    l_fwd(2, 0)
+
+    copy(st_in.at[pl.ds(1, 31)], st_in.at[pl.ds(1, 31)], t_s, t_r, sib).wait_recv()
 
     def st_mean(t, total):
-        tc(t).wait_recv()
         return total + st_in[t]
 
     mean_g = lax.fori_loop(1, 32, st_mean, st_out[...])[0:1] * (1.0 / 32.0)
@@ -440,35 +438,32 @@
         v = (v - mean_c) * rs_c * gain_c + shift_c
         return v / (1.0 + jnp.exp(-v))
 
+    def act_rows(p, _):
+        v = activate(feat[p].astype(F32))
+        act[2 * p + 1, 8 : 8 + C, :] = v[0:C]
+        act[2 * p + 2, 8 : 8 + C, :] = v[C : 2 * C]
+        return 0
+
     f_done(1)
     l_send(1, 2)
     f_done(2)
     l_send(2, 2)
-    l_fwd(1, 0)
-    l_fwd(2, 0)
-    s_send(1, 0)
-    s_send(2, 0)
-    l_other(0)
-    s_send(0, 1, 3)
-
-    def act_rows(p, _):
-        v = activate(feat[p].astype(F32))
-        act[2 * p + 1, 8 : 8 + C, :] = v[0:C]
-        act[2 * p + 2, 8 : 8 + C, :] = v[C : 2 * C]
-        return 0
-
     lax.fori_loop(0, 5, act_rows, 0)
-    l_fwd(1, 1, 3)
-    l_fwd(2, 1, 3)
     zin(3).wait_recv()
     l_send(3, 0)
     f_send(3)
+    s_send(1, 0)
+    s_send(2, 0)
+    l_fwd(1, 1, 3)
+    l_fwd(2, 1, 3)
+    l_other(0)
+    s_send(0, 1, 3)
     lax.fori_loop(5, 10, act_rows, 0)
-    l_last(0)
-    s_send(0, 2)
     f_fwd(3)
     l_send(3, 1)
     l_send(3, 3)
+    l_last(0)
+    s_send(0, 2)
     l_fwd(1, 2)
     l_fwd(2, 2)
 
@@ -597,27 +592,11 @@
 
     lax.fori_loop(0, R, finish, 0)
 
-    for i in range(3):
-        zc(i).wait_send()
-
-    @pl.when(first)
-    def _():
-        f_sent(0)
-
-    for k in range(1, 4):
-        f_sent(k)
-    for k in range(4):
-        l_sent(k)
-        for w in range(4):
-            sc(k, w, core).wait_send()
+    for blk in (wall.at[0], wall.at[1, pl.ds(0, 3)], wall.at[1, 3, pl.ds(0, 3)]):
+        copy(blk, blk, w_s, z_r.at[0], sib).wait_send()
     for c in hcs:
         c.wait_send()
-
-    def st_sent(t, _):
-        tc(t).wait_send()
-        return 0
-
-    lax.fori_loop(1, 32, st_sent, 0)
+    copy(st_in.at[pl.ds(1, 31)], st_in.at[pl.ds(1, 31)], t_s, t_r, sib).wait_send()
 
 
 def local(features, hole_mask, norm_gain, norm_shift, conv_weight, mask_weight, conv_bias):
@@ -634,6 +613,7 @@
             pltpu.VMEM((22, STRIDE, CH), F32),
             pltpu.VMEM((3, 42 * C, CH), BF),
             pltpu.VMEM((R * C, CH), F32),
+            pltpu.VMEM((R, C), jnp.int32),
             pltpu.VMEM((R // 2, 2 * C, CH), BF),
             pltpu.VMEM((2, 24, CH), F32),
             pltpu.VMEM((2, 2 * C, CH), BF),
@@ -646,17 +626,15 @@
             pltpu.VMEM((128, CH), F32),
             pltpu.VMEM((8, 128), F32),
             pltpu.VMEM((32, 8, 128), F32),
-            dma((3,)), dma((3,)),
-            dma((4, 2)), dma((4, 2)), dma((4, 2)), dma((4, 2)),
-            dma((4, 4, 2)), dma((4, 4, 2)), dma((4, 4)), dma((4, 4)),
-            dma((4, 4)), dma((4, 4)), dma((16,)), dma((16,)), dma((32,)), dma((32,)), dma(()),
+            dma(()), dma((3,)), dma((4, 2)), dma((4, 2)), dma((4, 4, 2)), dma((4, 4)), dma((4,)),
+            dma((16,)), dma((8,)), dma(()), dma(()), dma(()), dma(()),
             pltpu.VMEM((R, C, CH), BF),
         ],
         compiler_params=pltpu.CompilerParams(
             collective_id=0, has_side_effects=True, vmem_limit_bytes=56 << 20
         ),
         name="conv",
-    )(features, hole_mask, norm_gain, norm_shift, conv_weight, mask_weight, conv_bias)
+    )(features, hole_mask.reshape(R, 1, C), norm_gain, norm_shift, conv_weight, mask_weight, conv_bias)
     return result
 
 

time: 78.4 us -> 72.8 us (0.929)
  Pallas kernels: 74.4 us -> 70.4 us
  local copies, waits for them, and re-layouts: 3.56 us -> 2.26 us
    pallas_call x1, Pallas kernels: 74.4 us -> 70.4 us  [local(): pl.pallas_call(kernel, out_shape=jax.ShapeDtypeStruct((1, R, C, CH), BF),...]
    unnamed x2 -> x1, local copies, waits for them, and re-layouts: 3.56 us -> 2.26 us
where the time goes in v3:
time: 72.8 us; the launch traced here: 72.6 us
  Pallas kernels  70.4 us (97%)
  local copies, waits for them, and re-layouts  2.26 us (3%)
    pallas_call x1, Pallas kernels, local(): pl.pallas_call(kernel, out_shape=jax.ShapeDtypeStruct((1, R, C, CH), BF),...  70.4 us
    unnamed x1, local copies, waits for them, and re-layouts  2.26 us

profile of v3, /device:TPU:1, one launch (start us, length us, event | category | flops | bytes accessed | tf_op | source)
XLA Modules:
  0.0 72.6 jit_solution(17444822648023864444)
XLA Ops:
  0.0 70.4 %conv.1 = bf16[1,20,40,640]{3,2,1,0:T(8,128)(2,1)} custom-call(bf16[1,20,40,640]{3,2,1,0:T(8,128)(2,1)} %feat4.1, s32[20,1,40]{2,1,0:T(1,128)} %bitcast.1, f32[640]{0:T(1024)} %gain.1, f32[640]{0:T(1024)} %shift.1, bf16[9,40,640]{2,1,0:T(8,128)(2,1)} %weight.1, f32[9,640]{1,0:T(8,128)} %mask_w.1, f32[640]{0:T(1024)} %bias.1), custom_call_target="tpu_custom_call" | custom-call | tf_op jit(solution)/shard_map/conv/pallas_call | solution.py:605
  70.4 2.3 %copy.9 = bf16[1,20,40,640]{3,2,1,0:T(8,128)(2,1)} copy(bf16[1,20,40,640]{3,2,1,0:T(8,128)(2,1)} %conv.1) | data formatting | bytes 2048000

commit v4 on v3

--- a/solution.py
+++ b/solution.py
@@ -15,6 +15,7 @@
 CUT = 128
 STRIDE = 56
 DELTAS = (0, 3, 1, 2)
+DIRECT = (1, 2, 3)
 
 
 def dot(a, b):
@@ -58,7 +59,10 @@
     feat_in = pltpu.make_async_copy(feat4.at[0], feat_raw, in_sem)
     feat_in.start()
     barrier = pltpu.get_barrier_semaphore()
-    for d in far + yn:
+    x2, y2 = at(y, zh, (x + 2) % 4, core, col), at((y + 2) % 4, zh, x, core, col)
+    f2 = tuple(jnp.where(first, a, b) for a, b in zip(y2, x2))
+    l2 = tuple(jnp.where(first, b, a) for a, b in zip(y2, x2))
+    for d in far + yn + [y2]:
         pl.semaphore_signal(barrier, inc=1, device_id=d, device_id_type=MESH)
 
     def peer(t):
@@ -114,12 +118,11 @@
             wall[1, zh, y, j, 224:240, :] = jnp.zeros((16, 128), BF)
 
     def clear(t, _):
-        for k in range(4):
-            wm[k, t] = jnp.zeros((256, CH), BF)
+        wm[t, 160:288] = jnp.zeros((128, CH), BF)
         return 0
 
     lax.fori_loop(0, 9, clear, 0)
-    pl.semaphore_wait(barrier, 36)
+    pl.semaphore_wait(barrier, 37)
 
     def copy(src, dst, s, r, d):
         return pltpu.make_async_remote_copy(src, dst, s, r, device_id=d, device_id_type=MESH)
@@ -155,19 +158,34 @@
         blk = wall.at[which, zof[k], (l_there + w) % 4]
         return copy(blk, blk, w_s, c_r.at[k], sib)
 
+    def f2c(k, who):
+        blk = wall.at[core, zof[k], lme, (fme + who) % 4]
+        return copy(blk, blk, w_s, fh_r.at[k, 0], f2)
+
+    def l2c(k, e, who):
+        blk = wall.at[core, zof[k], (lme + who) % 4, (fme + e) % 4]
+        return copy(blk, blk, w_s, q_r.at[k, e], l2)
+
     def f_send(k):
         fc(k, 0, 0).start()
         fc(k, 1, 0).start()
+        if k in DIRECT:
+            f2c(k, 0).start()
 
     def f_fwd(k):
         fc(k, 0, 3).wait_recv()
-        fhc(k, 0, 3).start()
+        if k not in DIRECT:
+            fhc(k, 0, 3).start()
         fc(k, 1, 1).wait_recv()
-        fhc(k, 1, 1).start()
+        if k not in DIRECT:
+            fhc(k, 1, 1).start()
 
     def f_done(k):
-        fhc(k, 0, 2).wait_recv()
-        fhc(k, 1, 2).wait_recv()
+        if k in DIRECT:
+            f2c(k, 2).wait_recv()
+        else:
+            fhc(k, 0, 2).wait_recv()
+            fhc(k, 1, 2).wait_recv()
 
     def on(k, e, cond_fn):
         if k == 0 and e == 0:
@@ -178,13 +196,16 @@
     def l_send(k, e):
         pc(k, e, 0, 0).start()
         pc(k, e, 1, 0).start()
+        if k in DIRECT:
+            l2c(k, e, 0).start()
 
     def l_fwd(k, *es):
         for e in es:
             def go(e=e):
                 i, who = (0, 3) if e < 2 else (1, 1)
                 pc(k, e, i, who).wait_recv()
-                qc(k, e, who).start()
+                if k not in DIRECT:
+                    qc(k, e, who).start()
             on(k, e, go)
 
     def l_other(k):
@@ -196,7 +217,7 @@
 
     def l_last(k):
         for e in range(4):
-            on(k, e, lambda e=e: qc(k, e, 2).wait_recv())
+            on(k, e, lambda e=e: (l2c if k in DIRECT else qc)(k, e, 2).wait_recv())
 
     def s_send(k, *ws):
         for w in ws:
@@ -223,7 +244,9 @@
     old = lax.broadcasted_iota(jnp.int32, (CH, 128), 0)
     shift_by = jnp.zeros((CH, 128), jnp.int32)
     for i in range(16):
-        j = (i % 4) * 4 + i // 4
+        d = (i % 4 - zh + 4) % 4
+        k = jnp.where(d == 0, 0, jnp.where(d == 3, 1, jnp.where(d == 1, 2, 3)))
+        j = k * 4 + i // 4
         shift_by = jnp.where(old >= 40 * i, 40 * (j - i), shift_by)
     target = old + shift_by
     lane0 = lax.broadcasted_iota(jnp.int32, (CH, 128), 1)
@@ -408,8 +431,6 @@
     l_send(2, 1)
     l_send(2, 3)
     l_fwd(0, 2)
-    l_fwd(1, 0)
-    l_fwd(2, 0)
 
     copy(st_in.at[pl.ds(1, 31)], st_in.at[pl.ds(1, 31)], t_s, t_r, sib).wait_recv()
 
@@ -454,8 +475,6 @@
     f_send(3)
     s_send(1, 0)
     s_send(2, 0)
-    l_fwd(1, 1, 3)
-    l_fwd(2, 1, 3)
     l_other(0)
     s_send(0, 1, 3)
     lax.fori_loop(5, 10, act_rows, 0)
@@ -464,13 +483,11 @@
     l_send(3, 3)
     l_last(0)
     s_send(0, 2)
-    l_fwd(1, 2)
-    l_fwd(2, 2)
 
     for c in hcs[:8]:
         c.wait_recv()
-    act[0, 8 : 8 + C, :] = jnp.where(row > 0, activate(row_in[0, 40:80].astype(F32)), 0.0)
-    act[21, 8 : 8 + C, :] = jnp.where(row < 7, activate(row_in[1, 0:40].astype(F32)), 0.0)
+    act[0, 8 : 8 + C, :] = jnp.where(row > 0, activate(row_in[0].astype(F32)[40:80]), 0.0)
+    act[21, 8 : 8 + C, :] = jnp.where(row < 7, activate(row_in[1].astype(F32)[0:40]), 0.0)
     for side, there, off in ((0, col > 0, 7), (1, col < 3, 48)):
         edge = jnp.where(there, activate(col_in[side]), 0.0)
         for r in range(R):
@@ -487,7 +504,6 @@
     f_done(3)
     l_send(3, 2)
     s_send(3, 0)
-    l_fwd(3, 0)
 
     def fill(p, _):
             r = jnp.where(p < 11, 2 * p, 2 * p - 21)
@@ -498,24 +514,18 @@
                 taps[dx, pl.ds(pl.multiple_of(80 * p, 80), 80), :] = v
             return 0
 
-    lax.fori_loop(0, 11, fill, 0)
-    l_other(1)
-    s_send(1, 1, 3)
-    l_other(2)
-    s_send(2, 1, 3)
-    lax.fori_loop(11, 21, fill, 0)
-    l_fwd(3, 1, 3)
+    lax.fori_loop(0, 21, fill, 0)
 
     low_half = lax.broadcasted_iota(jnp.int32, (16, 128), 0) < 8
 
     def delta(k):
         return jnp.where(k == 0, 0, jnp.where(k == 1, 3, jnp.where(k == 2, 1, 2)))
 
-    def merge(k):
+    def merge(k, _):
         z = lax.rem(zh + delta(k), 4)
 
         for m in range(2):
-            base = pl.multiple_of(32 * z + 80 * m, 16)
+            base = pl.multiple_of(jnp.where(k == 0, 0, 128 + 160 * k) + 80 * m, 16)
             rows = pl.ds(base, 80)
             ya, yb = 2 * m, 2 * m + 1
 
@@ -531,10 +541,10 @@
                     mid_s = jnp.where(low_half, a2, b2).astype(BF)
                     mid_t = jnp.concatenate([a2[8:16], b2[0:8]], axis=0).astype(BF)
                     ln = pl.ds(128 * n, 128)
-                    wm[k, 2 * j, rows, ln] = jnp.concatenate(
+                    wm[2 * j, rows, ln] = jnp.concatenate(
                         [a[0:32, :], mid_s, b[0:32, :]], axis=0
                     )
-                    wm[k, 2 * j + 1, rows, ln] = jnp.concatenate(
+                    wm[2 * j + 1, rows, ln] = jnp.concatenate(
                         [a[48:80, :], mid_t, b[48:80, :]], axis=0
                     )
                 return 0
@@ -547,20 +557,29 @@
 
             for n in range(5):
                 mid = jnp.where(low_half, tile(ya, n, 2).astype(F32), tile(yb, n, 0).astype(F32))
-                wm[k, 8, rows, pl.ds(128 * n, 128)] = jnp.concatenate(
+                wm[8, rows, pl.ds(128 * n, 128)] = jnp.concatenate(
                     [tile(ya, n, 0), tile(ya, n, 1), mid.astype(BF), tile(yb, n, 1), tile(yb, n, 2)],
                     axis=0,
                 )
-
-    def conv(k, dy):
-        win = pl.ds(pl.multiple_of(128 * lax.rem(zh + delta(k), 4), 128), 256)
+        return 0
+
+    def conv(w, dy):
+        lane_at = jnp.where(w == 0, 0, jnp.where(w == 1, 128, 384))
+        win = pl.ds(pl.multiple_of(lane_at, 128), 256)
         start = pl.multiple_of(jnp.where(dy == 0, 0, jnp.where(dy == 1, 880, 80)), 80)
         parts = [taps[dx, pl.ds(start, R * C), win] for dx in range(3)]
-        rhs = wm[k, pl.ds(3 * dy, 3)].reshape(768, CH)
+        rhs = wm[pl.ds(3 * dy, 3), pl.ds(pl.multiple_of(256 * w, 256), 256), :].reshape(768, CH)
         acc[...] += dot(jnp.concatenate(parts, axis=1), rhs)
 
+    def arrive(k):
+        l_fwd(k, 0, 1, 3, 2)
+        l_other(k)
+        s_send(k, 1, 3)
+        l_last(k)
+        s_send(k, 2)
+
     def step(t, _):
-        k, dy = t // 3, lax.rem(t, 3)
+        w, dy = t // 3, lax.rem(t, 3)
 
         def when(there, *fs):
             @pl.when(t == there)
@@ -568,24 +587,24 @@
                 for f in fs:
                     f()
 
-        for kk in range(4):
-            when(3 * kk, lambda kk=kk: s_wait(kk))
+        when(0, lambda: s_wait(0))
+        when(1, lambda: arrive(1))
+        when(2, lambda: arrive(2))
+        when(3, lambda: s_wait(1), lambda: s_wait(2))
+        when(4, lambda: arrive(3))
+        when(6, lambda: s_wait(3))
 
         @pl.when(dy == 0)
         def _():
-            merge(k)
-
-        conv(k, dy)
-        when(
-            0,
-            lambda: l_last(1), lambda: s_send(1, 2), lambda: l_last(2), lambda: s_send(2, 2),
-            lambda: l_fwd(3, 2),
-        )
-        when(2, lambda: l_other(3), lambda: s_send(3, 1, 3))
-        when(3, lambda: l_last(3), lambda: s_send(3, 2))
-        return 0
-
-    lax.fori_loop(0, 12, step, 0)
+            lo = jnp.where(w == 0, 0, jnp.where(w == 1, 1, 3))
+            hi = jnp.where(w == 0, 1, jnp.where(w == 1, 3, 4))
+            lax.fori_loop(lo, hi, merge, 0)
+
+        conv(w, dy)
+        return 0
+
+    lax.fori_loop(0, 9, step, 0)
+
     def finish(r, _):
         out4[0, r] = acc[pl.ds(pl.multiple_of(C * r, 8), C), :].astype(BF)
         return 0
@@ -609,7 +628,7 @@
         out_specs=vm,
         scratch_shapes=[
             pltpu.VMEM((2, 4, 4, 4, BLK, 128), BF),
-            pltpu.VMEM((4, 9, 256, CH), BF),
+            pltpu.VMEM((9, 768, CH), BF),
             pltpu.VMEM((22, STRIDE, CH), F32),
             pltpu.VMEM((3, 42 * C, CH), BF),
             pltpu.VMEM((R * C, CH), F32),

time: 72.8 us -> 68.1 us (0.935)
  Pallas kernels: 70.4 us -> 65.7 us
    pallas_call x1, Pallas kernels: 70.4 us -> 65.7 us  [local(): pl.pallas_call(kernel, out_shape=jax.ShapeDtypeStruct((1, R, C, CH), BF),...]
where the time goes in v4:
time: 68.1 us; the launch traced here: 68 us
  Pallas kernels  65.7 us (96%)
  local copies, waits for them, and re-layouts  2.26 us (3%)
    pallas_call x1, Pallas kernels, local(): pl.pallas_call(kernel, out_shape=jax.ShapeDtypeStruct((1, R, C, CH), BF),...  65.7 us
    unnamed x1, local copies, waits for them, and re-layouts  2.26 us

profile of v4, /device:TPU:1, one launch (start us, length us, event | category | flops | bytes accessed | tf_op | source)
XLA Modules:
  0.0 68.0 jit_solution(7531875382953230243)
XLA Ops:
  0.0 65.7 %conv.1 = bf16[1,20,40,640]{3,2,1,0:T(8,128)(2,1)} custom-call(bf16[1,20,40,640]{3,2,1,0:T(8,128)(2,1)} %feat4.1, s32[20,1,40]{2,1,0:T(1,128)} %bitcast.1, f32[640]{0:T(1024)} %gain.1, f32[640]{0:T(1024)} %shift.1, bf16[9,40,640]{2,1,0:T(8,128)(2,1)} %weight.1, f32[9,640]{1,0:T(8,128)} %mask_w.1, f32[640]{0:T(1024)} %bias.1), custom_call_target="tpu_custom_call" | custom-call | tf_op jit(solution)/shard_map/conv/pallas_call | solution.py:624
  65.7 2.3 %copy.9 = bf16[1,20,40,640]{3,2,1,0:T(8,128)(2,1)} copy(bf16[1,20,40,640]{3,2,1,0:T(8,128)(2,1)} %conv.1) | data formatting | bytes 2048000

commit v5 on v4

--- a/solution.py
+++ b/solution.py
@@ -588,9 +588,8 @@
                     f()
 
         when(0, lambda: s_wait(0))
-        when(1, lambda: arrive(1))
-        when(2, lambda: arrive(2))
-        when(3, lambda: s_wait(1), lambda: s_wait(2))
+        when(2, lambda: arrive(1))
+        when(3, lambda: arrive(2), lambda: s_wait(1), lambda: s_wait(2))
         when(4, lambda: arrive(3))
         when(6, lambda: s_wait(3))
 

time: 68.1 us -> 69.1 us (1.015)
  Pallas kernels: 65.7 us -> 66.7 us
    pallas_call x1, Pallas kernels: 65.7 us -> 66.7 us  [local(): pl.pallas_call(kernel, out_shape=jax.ShapeDtypeStruct((1, R, C, CH), BF),...]
where the time goes in v5:
time: 69.1 us; the launch traced here: 69 us
  Pallas kernels  66.7 us (97%)
  local copies, waits for them, and re-layouts  2.26 us (3%)
    pallas_call x1, Pallas kernels, local(): pl.pallas_call(kernel, out_shape=jax.ShapeDtypeStruct((1, R, C, CH), BF),...  66.7 us
    unnamed x1, local copies, waits for them, and re-layouts  2.26 us

profile of v5, /device:TPU:1, one launch (start us, length us, event | category | flops | bytes accessed | tf_op | source)
XLA Modules:
  0.0 69.0 jit_solution(12417317713094543667)
XLA Ops:
  0.0 66.7 %conv.1 = bf16[1,20,40,640]{3,2,1,0:T(8,128)(2,1)} custom-call(bf16[1,20,40,640]{3,2,1,0:T(8,128)(2,1)} %feat4.1, s32[20,1,40]{2,1,0:T(1,128)} %bitcast.1, f32[640]{0:T(1024)} %gain.1, f32[640]{0:T(1024)} %shift.1, bf16[9,40,640]{2,1,0:T(8,128)(2,1)} %weight.1, f32[9,640]{1,0:T(8,128)} %mask_w.1, f32[640]{0:T(1024)} %bias.1), custom_call_target="tpu_custom_call" | custom-call | tf_op jit(solution)/shard_map/conv/pallas_call | solution.py:623
  66.7 2.3 %copy.9 = bf16[1,20,40,640]{3,2,1,0:T(8,128)(2,1)} copy(bf16[1,20,40,640]{3,2,1,0:T(8,128)(2,1)} %conv.1) | data formatting | bytes 2048000
